TPU v7x, 32 devices: a whole 2x2x4 slice. The times are simulated.
32 devices in a mesh: ctx: 8 (over z, y), fsdp: 4 (over x, core).
Axes of the slice: x: 2, y: 2, z: 4, core: 2. Of those that a mesh axis runs over, the one named last changes fastest.
Arguments:
- tokens: bfloat16 [4, 2048, 1024], P('fsdp', 'ctx'), may hold values from -6 to 6
- cotangent: bfloat16 [4, 2048, 1024], P('fsdp', 'ctx'), may hold values from -6 to 6
- positions: int32 [4, 2048], P('fsdp', 'ctx'), may hold values from 0 to 4095, as said below
- block_order: int32 [4, 16], P('fsdp'), may hold values from 0 to 15, as said below
- joint_weight: bfloat16 [1024, 3072], P('fsdp'), may hold values from -0.1875 to 0.1875
- joint_bias: bfloat16 [3072], P('fsdp'), may hold values from -3 to 3
- dense_weight: bfloat16 [1024, 1024], P('fsdp'), may hold values from -4 to 4
- dense_bias: bfloat16 [1024], P('fsdp'), may hold values from -2 to 2
- inner_weight: bfloat16 [1024, 4096], P('fsdp'), may hold values from -0.1875 to 0.1875
- inner_bias: bfloat16 [4096], P('fsdp'), may hold values from -3 to 3
- outer_weight: bfloat16 [4096, 1024], P('fsdp'), may hold values from -0.09375 to 0.09375
- outer_bias: bfloat16 [1024], P('fsdp'), may hold values from -2 to 2
- attention_gain: bfloat16 [1024], P('fsdp'), may hold values from 0.5 to 1.5
- attention_shift: bfloat16 [1024], P('fsdp'), may hold values from -2 to 2
- feedforward_gain: bfloat16 [1024], P('fsdp'), may hold values from 0.5 to 1.5
- feedforward_shift: bfloat16 [1024], P('fsdp'), may hold values from -2 to 2
Outputs:
- layer_output: bfloat16 [4, 2048, 1024], P('fsdp', 'ctx')
- tokens_grad: bfloat16 [4, 2048, 1024], P('fsdp', 'ctx')
- joint_weight_grad: float32 [1024, 3072], P('fsdp')
- joint_bias_grad: float32 [3072], P('fsdp')
- dense_weight_grad: float32 [1024, 1024], P('fsdp')
- dense_bias_grad: float32 [1024], P('fsdp')
- inner_weight_grad: float32 [1024, 4096], P('fsdp')
- inner_bias_grad: float32 [4096], P('fsdp')
- outer_weight_grad: float32 [4096, 1024], P('fsdp')
- outer_bias_grad: float32 [1024], P('fsdp')
- attention_gain_grad: float32 [1024], P('fsdp')
- attention_shift_grad: float32 [1024], P('fsdp')
- feedforward_gain_grad: float32 [1024], P('fsdp')
- feedforward_shift_grad: float32 [1024], P('fsdp')
Inputs may be any that keep to these rules, and one draw needn't show every extreme that they name: `block_order`: row i lists, for the 16 stored blocks of 128 tokens of sequence i, the causal block that each holds; every number of 0 to 15 stands once in a row. `positions`: the token of causal index j has rotary position 2 j or 2 j + 1.
All inputs are finite; a program needn't handle non-finite values.
Results may differ from a plain program's by a relative error of at most 0.018.
Values may be sent and summed in bfloat16 or wider, within the bound.
No kernel may reach another device: no remote copies, remote signals or barrier semaphores. Data moves between devices by JAX's collectives and lax.ppermute only.
A program may use at most 384 MiB of HBM per device.

v0:
```python
import functools
import math

import jax
import jax.numpy as jnp
from jax import lax
from jax.experimental import pallas as pl
from jax.experimental.pallas import tpu as pltpu
from jax.sharding import PartitionSpec as P

D = 1024
H = 16
DH = 64
ROT = 16
PAIR = 2 * DH
EPSILON = 1e-05
MASKED = -1e30
SCALE = DH ** (-0.5)
LOG2E = math.log2(math.e)
BF16 = jnp.bfloat16
F32 = jnp.float32
MIB = 1024 * 1024


def dot(left, right, left_dim=1, right_dim=0):
    return lax.dot_general(
        left, right, (((left_dim,), (right_dim,)), ((), ())), preferred_element_type=F32
    )


def ring_order(count):
    return list(range(0, count, 2)) + list(range(1, count, 2))[::-1]


def ring_steps(axis, count):
    order = ring_order(count)
    onward = [(order[k], order[(k + 1) % count]) for k in range(count)]
    back = [(b, a) for a, b in onward]
    places = [0] * count
    for place, index in enumerate(order):
        places[index] = place
    place = jnp.array(places, jnp.int32)[lax.axis_index(axis)]
    return onward, back, place


def ring_reduce(pick, axis, count):
    onward, back, place = ring_steps(axis, count)
    half = count // 2
    far = pick((place + half) % count)
    rows = far.shape[0] // 2
    up = lax.ppermute(far[:rows], axis, onward)
    down = lax.ppermute(far[rows:], axis, back)
    for step in range(2, half + 1):
        mine_up = pick((place + half - step + 1) % count)
        mine_down = pick((place + count - half + step - 1) % count)
        if step == 2:
            mine_up = jnp.concatenate([mine_up[:rows] + up, mine_up[rows:]], axis=0)
            mine_down = jnp.concatenate([mine_down[:rows], mine_down[rows:] + down], axis=0)
        else:
            mine_up = mine_up + up
            mine_down = mine_down + down
        up = lax.ppermute(mine_up, axis, onward)
        down = lax.ppermute(mine_down, axis, back)
    own = pick(place).astype(F32)
    return (own + up.astype(F32) + down.astype(F32)).astype(BF16)


def ring_gather(own, axis, count, place_chunk, state, zero=0):
    onward, back, place = ring_steps(axis, count)
    half = count // 2
    rows = own.shape[0] // 2
    state = place_chunk(state, own, place, 0)
    up = down = own
    for step in range(1, half):
        up = lax.ppermute(up, axis, onward)
        down = lax.ppermute(down, axis, back)
        state = place_chunk(state, up, (place + count - step) % count, 0)
        state = place_chunk(state, down, (place + step) % count, 0)
    up = lax.ppermute(lax.dynamic_slice_in_dim(up, zero, rows, 0), axis, onward)
    down = lax.ppermute(lax.dynamic_slice_in_dim(down, zero + rows, rows, 0), axis, back)
    return place_chunk(state, jnp.concatenate([up, down], axis=0), (place + half) % count, 0)


def nothing(array):
    value = array.reshape(-1)[0].astype(jnp.int32)
    return jnp.minimum(jnp.abs(value), 0)


def gather_pairs(own, count):
    if count != 4:
        return lax.all_gather(own, "fsdp", axis=0)
    index = lax.axis_index("fsdp")
    across = lax.ppermute(own, "fsdp", [(k, k ^ 2) for k in range(4)])
    first = index < 2
    pair = jnp.stack([jnp.where(first, own, across), jnp.where(first, across, own)])
    other = lax.ppermute(pair, "fsdp", [(k, k ^ 1) for k in range(4)])
    even = index % 2 == 0
    return jnp.stack([jnp.where(even, pair, other), jnp.where(even, other, pair)], axis=1).reshape(
        (4,) + own.shape
    )


def columns_for_rows(weight, count, zero, later):
    rows, columns = weight.shape
    part = columns // count
    if count != 4:
        parts = weight.reshape(rows, count, part).transpose(1, 0, 2)
        return lax.all_to_all(parts, "fsdp", 0, 0).reshape(count * rows, part)
    index = lax.axis_index("fsdp")
    chip, core = index // 2, index % 2
    mine = lax.dynamic_slice_in_dim(weight, chip * 2 * part, 2 * part, 1)
    theirs = lax.dynamic_slice_in_dim(weight, (1 - chip) * 2 * part + zero, 2 * part, 1)
    across = lax.ppermute(theirs, "fsdp", [(k, k ^ 2) for k in range(4)])
    low = chip == 0
    pair = jnp.stack([jnp.where(low, mine, across), jnp.where(low, across, mine)])
    even = core == 0
    other = lax.ppermute(
        lax.dynamic_slice_in_dim(pair, (1 - core) * part + later, part, 2),
        "fsdp",
        [(k, k ^ 1) for k in range(4)],
    )
    kept = lax.dynamic_slice_in_dim(pair, core * part, part, 2)
    return jnp.stack(
        [jnp.where(even, kept, other), jnp.where(even, other, kept)], axis=1
    ).reshape(count * rows, part)


def turn(heads, cosine, sine):
    lane = lax.broadcasted_iota(jnp.int32, heads.shape, 1) % DH
    partner = jnp.where(
        lane < ROT // 2,
        pltpu.roll(heads, PAIR - ROT // 2, 1),
        pltpu.roll(heads, ROT // 2, 1),
    )
    return heads * cosine + partner * sine


def project_kernel(tokens_ref, upstream_ref, params_ref, weight_ref, bias_ref, dense_ref, cos_ref,
                   sin_ref, out_ref, attn_ref, ff_ref, normed_ref):
    @pl.when(pl.program_id(1) == 0)
    def norm():
        inputs = tokens_ref[0, 0].astype(F32)
        centered = inputs - jnp.mean(inputs, axis=-1, keepdims=True)
        variance = jnp.mean(centered * centered, axis=-1, keepdims=True)
        normed = centered * lax.rsqrt(variance + EPSILON)
        normed_ref[...] = normed.astype(BF16)
        attn_ref[...] = (normed * params_ref[0:1] + params_ref[1:2]).astype(BF16)
        ff_ref[...] = (normed * params_ref[2:3] + params_ref[3:4]).astype(BF16)

    joint = dot(attn_ref[...], weight_ref[...]) + bias_ref[...].astype(F32)
    low = lax.broadcasted_iota(jnp.int32, (joint.shape[0], PAIR), 1) < DH
    one, two, three = joint[:, :PAIR], joint[:, PAIR : 2 * PAIR], joint[:, 2 * PAIR :]
    query = jnp.where(low, one, two)
    key = pltpu.roll(jnp.where(low, three, one), DH, 1)
    value = jnp.where(low, two, three)
    cosine, sine = cos_ref[...], sin_ref[...]
    out_ref[0, :, :PAIR] = turn(query, cosine, sine).astype(BF16)
    out_ref[0, :, PAIR : 2 * PAIR] = turn(key, cosine, sine).astype(BF16)
    out_ref[0, :, 2 * PAIR : 3 * PAIR] = value.astype(BF16)
    out_ref[0, :, 3 * PAIR :] = dot(upstream_ref[0, 0], dense_ref[...], 1, 1).astype(BF16)


def project(both, params, weight, bias, dense, cosine, sine, seqs, tokens, pairs):
    wide = jax.ShapeDtypeStruct((seqs * tokens, D), BF16)
    rows = pl.BlockSpec((tokens, D), lambda s, p: (s, 0))
    return pl.pallas_call(
        project_kernel,
        grid=(seqs, pairs),
        in_specs=[
            pl.BlockSpec((1, 1, tokens, D), lambda s, p: (s, 0, 0, 0)),
            pl.BlockSpec((1, 1, tokens, D), lambda s, p: (s, 1, 0, 0)),
            pl.BlockSpec((4, D), lambda s, p: (0, 0)),
            pl.BlockSpec((D, 3 * PAIR), lambda s, p: (0, p)),
            pl.BlockSpec((1, 3 * PAIR), lambda s, p: (0, p)),
            pl.BlockSpec((PAIR, D), lambda s, p: (p, 0)),
            pl.BlockSpec((tokens, PAIR), lambda s, p: (s, 0)),
            pl.BlockSpec((tokens, PAIR), lambda s, p: (s, 0)),
        ],
        out_specs=[
            pl.BlockSpec((1, tokens, 4 * PAIR), lambda s, p: (s * pairs + p, 0, 0)),
            rows,
            rows,
            rows,
        ],
        out_shape=[
            jax.ShapeDtypeStruct((seqs * pairs, tokens, 4 * PAIR), BF16), wide, wide, wide,
        ],
        compiler_params=pltpu.CompilerParams(vmem_limit_bytes=40 * MIB),
        cost_estimate=pl.CostEstimate(
            flops=3 * seqs * pairs * tokens * D * 4 * PAIR,
            bytes_accessed=16 * MIB,
            transcendentals=0,
        ),
        name="project",
    )(both, both, params, weight, bias, dense, cosine, sine)


def unturn_kernel(back_ref, cos_ref, sin_ref, first_ref, grad_ref, mixed_ref):
    cosine, sine = cos_ref[...], sin_ref[...]
    query = turn(back_ref[0, :, PAIR : 2 * PAIR].astype(F32), cosine, -sine)
    key = turn(back_ref[0, :, 2 * PAIR : 3 * PAIR].astype(F32), cosine, -sine)
    value = back_ref[0, :, 3 * PAIR :].astype(F32)
    low = lax.broadcasted_iota(jnp.int32, query.shape, 1) < DH
    key = pltpu.roll(key, DH, 1)
    grad_ref[:, :PAIR] = jnp.where(low, query, key).astype(BF16)
    grad_ref[:, PAIR : 2 * PAIR] = jnp.where(low, value, query).astype(BF16)
    grad_ref[:, 2 * PAIR :] = jnp.where(low, key, value).astype(BF16)
    mixed_ref[...] = back_ref[0, :, :PAIR]


def unturn(back, cosine, sine, first, seqs, tokens, pairs):
    return pl.pallas_call(
        unturn_kernel,
        grid=(seqs, pairs),
        in_specs=[
            pl.BlockSpec((1, tokens, 4 * PAIR), lambda s, p: (s * pairs + p, 0, 0)),
            pl.BlockSpec((tokens, PAIR), lambda s, p: (s, 0)),
            pl.BlockSpec((tokens, PAIR), lambda s, p: (s, 0)),
            pl.BlockSpec(memory_space=pl.ANY),
        ],
        out_specs=[
            pl.BlockSpec((tokens, 3 * PAIR), lambda s, p: (s, p)),
            pl.BlockSpec((tokens, PAIR), lambda s, p: (s, p)),
        ],
        out_shape=[
            jax.ShapeDtypeStruct((seqs * tokens, pairs * 3 * PAIR), BF16),
            jax.ShapeDtypeStruct((seqs * tokens, pairs * PAIR), BF16),
        ],
        compiler_params=pltpu.CompilerParams(vmem_limit_bytes=32 * MIB),
        cost_estimate=pl.CostEstimate(flops=8 * MIB, bytes_accessed=5 * MIB, transcendentals=0),
        name="unturn",
    )(back, cosine, sine, first)


def attend_kernel(tile, block, unrolled, order_ref, in_ref, first_ref, out_ref, sorted_ref, flipped_ref,
                  score_ref, prob_ref, mixed_ref, dq_ref, dk_ref, dv_ref):
    head = pl.program_id(0)
    length = in_ref.shape[0]
    tiles = length // tile
    blocks = length // block

    def loop(count, body, carry):
        if unrolled:
            for index in range(count):
                carry = body(index, carry)
            return carry
        return lax.fori_loop(0, count, body, carry)

    def span(index, size):
        start = index * size
        if not isinstance(start, int):
            start = pl.multiple_of(start, size)
        return pl.ds(start, size)

    @pl.when(head == 0)
    def prepare():
        def one(index, carry):
            sorted_ref[span(order_ref[index], block), :] = in_ref[span(index, block), :]
            return carry

        loop(blocks, one, 0)

        def flip(index, carry):
            flipped_ref[:, span(index, tile)] = sorted_ref[span(index, tile), :].T
            return carry

        loop(tiles, flip, 0)
        dk_ref[...] = jnp.zeros_like(dk_ref)
        dv_ref[...] = jnp.zeros_like(dv_ref)

    first = pl.multiple_of(head * DH, DH)

    def padded(rows):
        rows = rows.astype(F32)
        zero = jnp.zeros_like(rows)
        upper = jnp.where(head == 0, rows, zero)
        lower = jnp.where(head == 0, zero, rows)
        return jnp.concatenate([upper, lower], axis=0).astype(BF16)

    def one_tile(i, carry):
        query = padded(flipped_ref[pl.ds(first, DH), span(i, tile)])

        def score(j, top):
            part = dot(sorted_ref[span(j, tile), PAIR : 2 * PAIR], query)
            if not (unrolled and j < i):
                keys = j * tile + lax.broadcasted_iota(jnp.int32, part.shape, 0)
                queries = i * tile + lax.broadcasted_iota(jnp.int32, part.shape, 1)
                part = jnp.where(keys <= queries, part, MASKED)
            score_ref[span(j, tile), :] = part
            return jnp.maximum(top, jnp.max(part, axis=0, keepdims=True))

        top = loop(i + 1, score, jnp.full((1, tile), -3e38, F32))
        shift = top * (SCALE * LOG2E)

        def mix(j, status):
            total, mixed = status
            prob = jnp.exp2(score_ref[span(j, tile), :] * (SCALE * LOG2E) - shift)
            low = prob.astype(BF16)
            prob_ref[span(j, tile), :] = low
            total = total + jnp.sum(prob, axis=0, keepdims=True)
            values = flipped_ref[pl.ds(2 * PAIR + first, DH), span(j, tile)]
            return total, mixed + dot(values, low)

        total, mixed = loop(
            i + 1, mix, (jnp.zeros((1, tile), F32), jnp.zeros((DH, tile), F32))
        )
        inverse = 1.0 / total
        mixed = mixed * inverse
        mixed_ref[pl.ds(first, DH), span(i, tile)] = mixed
        grad = flipped_ref[pl.ds(3 * PAIR + first, DH), span(i, tile)].astype(F32) * inverse
        grad = grad.astype(BF16)
        delta = jnp.sum(grad.astype(F32) * mixed, axis=0, keepdims=True)
        grad = padded(grad)

        def pull(j, dq):
            low = prob_ref[span(j, tile), :]
            prob_grad = dot(sorted_ref[span(j, tile), 2 * PAIR : 3 * PAIR], grad)
            score_grad = (low.astype(F32) * (prob_grad - delta)).astype(BF16)
            dv_ref[span(j, tile), :] += dot(low, grad, 1, 1)
            dk_ref[span(j, tile), :] += dot(score_grad, query, 1, 1)
            keys = flipped_ref[pl.ds(PAIR + first, DH), span(j, tile)]
            return dq + dot(keys, score_grad)

        dq_ref[pl.ds(first, DH), span(i, tile)] = loop(i + 1, pull, jnp.zeros((DH, tile), F32))
        return carry

    loop(tiles, one_tile, 0)

    @pl.when(head == pl.num_programs(0) - 1)
    def finish():
        def one(index, carry):
            source = span(order_ref[index], block)
            target = span(index, block)
            out_ref[target, :PAIR] = mixed_ref[:, source].T.astype(BF16)
            out_ref[target, PAIR : 2 * PAIR] = (dq_ref[:, source].T * SCALE).astype(BF16)
            out_ref[target, 2 * PAIR : 3 * PAIR] = (dk_ref[source, :] * SCALE).astype(BF16)
            out_ref[target, 3 * PAIR :] = dv_ref[source, :].astype(BF16)
            return carry

        loop(blocks, one, 0)


def attend(order, packed, block, first):
    length = packed.shape[0]
    unrolled = length <= 2048
    tile = 256 if unrolled else 128
    return pl.pallas_call(
        functools.partial(attend_kernel, tile, block, unrolled),
        grid=(2,),
        in_specs=[
            pl.BlockSpec(memory_space=pltpu.SMEM),
            pl.BlockSpec(memory_space=pltpu.VMEM),
            pl.BlockSpec(memory_space=pl.ANY),
        ],
        out_specs=pl.BlockSpec(memory_space=pltpu.VMEM),
        out_shape=jax.ShapeDtypeStruct((length, 4 * PAIR), BF16),
        scratch_shapes=[
            pltpu.VMEM((length, 4 * PAIR), BF16),
            pltpu.VMEM((4 * PAIR, length), BF16),
            pltpu.VMEM((length, tile), F32),
            pltpu.VMEM((length, tile), BF16),
            pltpu.VMEM((PAIR, length), F32),
            pltpu.VMEM((PAIR, length), F32),
            pltpu.VMEM((length, PAIR), F32),
            pltpu.VMEM((length, PAIR), F32),
        ],
        compiler_params=pltpu.CompilerParams(
            vmem_limit_bytes=(40 if unrolled else 60) * MIB,
            dimension_semantics=("arbitrary",),
        ),
        cost_estimate=pl.CostEstimate(
            flops=56 * length * length * PAIR, bytes_accessed=4 * MIB, transcendentals=0
        ),
        name="attend",
    )(order, packed, first)


def feed_kernel(hidden_ref, inner_ref, bias_ref, outer_ref, upstream_ref,
                outer_grad_ref, inner_grad_ref, bias_grad_ref, out_ref, hidden_grad_ref):
    step = pl.program_id(0)
    hidden, upstream = hidden_ref[...], upstream_ref[...]
    inner = dot(hidden, inner_ref[...]) + bias_ref[...].astype(F32)
    share = 0.5 + 0.5 * lax.erf(inner * (0.5 ** 0.5))
    density = jnp.exp(inner * inner * -0.5) * (1.0 / math.sqrt(2.0 * math.pi))
    activated = (inner * share).astype(BF16)
    slope = share + inner * density
    inner_grad = (dot(upstream, outer_ref[...], 1, 1) * slope).astype(BF16)
    outer_grad_ref[...] = dot(activated, upstream, 0, 0).astype(BF16)
    inner_grad_ref[...] = dot(hidden, inner_grad, 0, 0).astype(BF16)
    bias_grad_ref[...] = jnp.sum(inner_grad.astype(F32), axis=0, keepdims=True)
    out = dot(activated, outer_ref[...])
    hidden_grad = dot(inner_grad, inner_ref[...], 1, 1)

    @pl.when(step == 0)
    def begin():
        out_ref[...] = out
        hidden_grad_ref[...] = hidden_grad

    @pl.when(step > 0)
    def add():
        out_ref[...] += out
        hidden_grad_ref[...] += hidden_grad


def feed(hidden, inner, bias, outer, upstream):
    tokens, columns = hidden.shape[0], inner.shape[1]
    tile = 256
    whole = pl.BlockSpec((tokens, D), lambda t: (0, 0))
    return pl.pallas_call(
        feed_kernel,
        grid=(columns // tile,),
        in_specs=[
            whole,
            pl.BlockSpec((D, tile), lambda t: (0, t)),
            pl.BlockSpec((1, tile), lambda t: (0, t)),
            pl.BlockSpec((tile, D), lambda t: (t, 0)),
            whole,
        ],
        out_specs=[
            pl.BlockSpec((tile, D), lambda t: (t, 0)),
            pl.BlockSpec((D, tile), lambda t: (0, t)),
            pl.BlockSpec((1, tile), lambda t: (0, t)),
            whole,
            whole,
        ],
        out_shape=[
            jax.ShapeDtypeStruct((columns, D), BF16),
            jax.ShapeDtypeStruct((D, columns), BF16),
            jax.ShapeDtypeStruct((1, columns), F32),
            jax.ShapeDtypeStruct((tokens, D), F32),
            jax.ShapeDtypeStruct((tokens, D), F32),
        ],
        compiler_params=pltpu.CompilerParams(vmem_limit_bytes=48 * MIB),
        cost_estimate=pl.CostEstimate(
            flops=0, bytes_accessed=0, transcendentals=0
        ),
        name="feed",
    )(hidden, inner, bias, outer, upstream)


def unpack_kernel(outer_rows, parts, in_ref, outer_ref, inner_ref):
    per = inner_ref.shape[0]
    width = in_ref.shape[2]
    outer_ref[...] = in_ref[0, :outer_rows].astype(F32)
    for part in range(parts):
        start = outer_rows + part * per
        inner_ref[:, part * width : (part + 1) * width] = in_ref[0, start : start + per].astype(F32)


def unpack(packed, outer_rows, parts):
    count, rows, width = packed.shape
    per = (rows - outer_rows) // parts
    if per % 16:
        outer = packed[:, :outer_rows].reshape(-1, width).astype(F32)
        inner = packed[:, outer_rows:].reshape(count, parts, per, width).transpose(0, 2, 1, 3)
        return outer, inner.reshape(count * per, -1).astype(F32)
    return pl.pallas_call(
        functools.partial(unpack_kernel, outer_rows, parts),
        grid=(count,),
        in_specs=[pl.BlockSpec((1, rows, width), lambda c: (c, 0, 0))],
        out_specs=[
            pl.BlockSpec((outer_rows, width), lambda c: (c, 0)),
            pl.BlockSpec((per, parts * width), lambda c: (c, 0)),
        ],
        out_shape=[
            jax.ShapeDtypeStruct((count * outer_rows, width), F32),
            jax.ShapeDtypeStruct((count * per, parts * width), F32),
        ],
        compiler_params=pltpu.CompilerParams(vmem_limit_bytes=16 * MIB),
        cost_estimate=pl.CostEstimate(flops=0, bytes_accessed=13 * MIB, transcendentals=0),
        name="unpack",
    )(packed)


def lay_out_kernel(parts, blocks, per, numbers_ref, *refs):
    count = len(refs) - 3
    joint_ref, dense_ref, vectors_ref = refs[count:]
    lanes = vectors_ref.shape[1]
    columns = parts * blocks
    for k in range(count):
        chunk_ref = refs[k]
        rows = pl.ds(pl.multiple_of(numbers_ref[k] * per, per), per)
        for c in range(columns):
            joint_ref[rows, c * lanes : (c + 1) * lanes] = chunk_ref[c * per : (c + 1) * per].astype(F32)
        first = columns * per
        for c in range(dense_ref.shape[1] // lanes):
            start = first + c * per
            dense_ref[rows, c * lanes : (c + 1) * lanes] = chunk_ref[start : start + per].astype(F32)
        first += dense_ref.shape[1] // lanes * per
        rows = pl.ds(pl.multiple_of(numbers_ref[k] * 16, 16), 16)
        vectors_ref[rows, :] = chunk_ref[first : first + 16].astype(F32)


def lay_out(numbers, chunks, parts, blocks, per, joint_shape, dense_shape):
    lanes = chunks[0].shape[1]
    whole = pl.BlockSpec(memory_space=pltpu.VMEM)
    return pl.pallas_call(
        functools.partial(lay_out_kernel, parts, blocks, per),
        in_specs=[pl.BlockSpec(memory_space=pltpu.SMEM)] + [whole] * len(chunks),
        out_specs=[whole] * 3,
        out_shape=[
            jax.ShapeDtypeStruct(joint_shape, F32),
            jax.ShapeDtypeStruct(dense_shape, F32),
            jax.ShapeDtypeStruct((16 * len(chunks), lanes), F32),
        ],
        compiler_params=pltpu.CompilerParams(vmem_limit_bytes=24 * MIB),
        cost_estimate=pl.CostEstimate(flops=0, bytes_accessed=6 * MIB, transcendentals=0),
        name="lay_out",
    )(numbers, *chunks)


def spread_out(part, ctx, each):
    if ctx > part.shape[0]:
        part = jnp.concatenate([part] * (ctx // part.shape[0]), axis=0)
    return lax.all_to_all(part.reshape((ctx, each) + part.shape[1:]), "ctx", 0, 0)


def rotary_tables(token_pos):
    lane = jnp.arange(PAIR, dtype=jnp.int32) % DH
    exponent = (2 * (lane % (ROT // 2))).astype(F32) / ROT
    inverse = 10000.0 ** (-exponent)
    phases = token_pos[:, None] * inverse[None, :]
    turned = (lane < ROT)[None, :]
    sign = jnp.where(lane < ROT // 2, -1.0, 1.0)[None, :]
    return jnp.where(turned, jnp.cos(phases), 1.0), jnp.where(turned, jnp.sin(phases) * sign, 0.0)


def per_device(ctx, fsdp, tokens, cotangent, positions, block_order, joint_weight, joint_bias,
               dense_weight, dense_bias, inner_weight, inner_bias, outer_weight, outer_bias,
               attention_gain, attention_shift, feedforward_gain, feedforward_shift):
    seqs = fsdp
    count = tokens.shape[1]
    block = count // 2
    rows = joint_weight.shape[0]
    heads = H // fsdp
    pairs = heads // 2
    joint_cols = heads * 3 * DH
    inner_cols = inner_weight.shape[1] // fsdp
    all_tokens = seqs * count
    me = lax.axis_index("ctx")

    pos = positions[0]
    table = block_order[0].astype(BF16)
    extra = jnp.stack(
        [
            attention_gain, attention_shift, feedforward_gain, feedforward_shift,
            dense_bias, outer_bias, (pos // 128).astype(BF16), (pos % 128).astype(BF16),
            jnp.pad(table, (0, rows - table.shape[0])),
        ]
    )
    extra = gather_pairs(jnp.pad(extra, ((0, 7), (0, 0))), fsdp).astype(F32)
    both = gather_pairs(jnp.concatenate([tokens, cotangent], axis=0), fsdp)
    joint_local = lax.all_to_all(
        joint_weight.reshape(rows, fsdp, joint_cols).transpose(1, 0, 2), "fsdp", 0, 0
    ).reshape(D, joint_cols)
    upstream = both[:, 1].reshape(all_tokens, D)

    params = extra[:, :4].transpose(1, 0, 2).reshape(4, D)
    bias_sum = (extra[:, 4] + extra[:, 5]).reshape(D)
    token_pos = (extra[:, 6] * 128.0 + extra[:, 7]).reshape(all_tokens)
    tables = extra[:, 8, : table.shape[0]].astype(jnp.int32)

    cosine, sine = rotary_tables(token_pos)

    sent, hidden_attn, hidden_ff, normed = project(
        both, params, joint_local, joint_bias[None], dense_weight, cosine, sine, seqs, count, pairs
    )
    jobs = seqs * pairs
    each = max(1, jobs // ctx)
    got = spread_out(sent, ctx, each)
    backs = []
    for k in range(each):
        sequence = (lax.rem(me, jobs) * each + k) // pairs
        order = lax.dynamic_index_in_dim(tables, sequence, 0, keepdims=False)
        out = attend(order, got[:, k].reshape(ctx * count, 4 * PAIR), block, sent)
        backs.append(out.reshape(ctx, count, 4 * PAIR))
    back = backs[0][:, None] if each == 1 else jnp.stack(backs, axis=1)
    inner_local = columns_for_rows(inner_weight, fsdp, nothing(got), nothing(back))

    outer_weight_grad, inner_weight_grad, inner_bias_grad, ff_out, hidden_ff_grad = feed(
        hidden_ff, inner_local, inner_bias[None], outer_weight, upstream
    )
    inner_bias_grad = inner_bias_grad[0]

    per = rows // ctx
    outer_rows = outer_weight.shape[0] // ctx
    inner_terms = inner_weight_grad.reshape(fsdp, ctx, per, inner_cols).transpose(1, 0, 2, 3)
    ff_terms = jnp.concatenate(
        [
            outer_weight_grad.reshape(ctx, outer_rows, D),
            inner_terms.reshape(ctx, fsdp * per, inner_cols),
        ],
        axis=1,
    )
    ff_own = lax.psum_scatter(ff_terms, "ctx", scatter_dimension=0)
    back = lax.all_to_all(back, "ctx", 0, 0)[: jobs // each].reshape(jobs, count, 4 * PAIR)
    joint_grad, mixed = unturn(back, cosine, sine, ff_terms, seqs, count, pairs)

    out_part = (ff_out + dot(mixed, dense_weight)).astype(BF16)
    hidden_attn_grad = dot(joint_grad, joint_local, 1, 1)
    e_part = (params[0] * hidden_attn_grad + params[2] * hidden_ff_grad).astype(BF16)
    parts = lax.all_to_all(
        jnp.concatenate([out_part.reshape(seqs, count, D), e_part.reshape(seqs, count, D)], axis=1),
        "fsdp", 0, 0,
    )

    dense_weight_grad = dot(mixed, upstream, 0, 0).astype(BF16)
    joint_weight_grad = dot(hidden_attn, joint_grad, 0, 0).astype(BF16)
    joint_bias_grad = jnp.sum(joint_grad.astype(F32), axis=0)
    upstream_grad = jnp.sum(upstream.astype(F32), axis=0)

    gains = jnp.stack(
        [
            jnp.sum(hidden_attn_grad * normed.astype(F32), axis=0),
            jnp.sum(hidden_attn_grad, axis=0),
            jnp.sum(hidden_ff_grad * normed.astype(F32), axis=0),
            jnp.sum(hidden_ff_grad, axis=0),
        ]
    ).astype(BF16)
    lanes = 2 * PAIR
    gains = gains.reshape(4, fsdp, ctx, per).transpose(2, 1, 0, 3).reshape(ctx, fsdp, 4 * per)
    gains = jnp.pad(gains, ((0, 0), (0, 0), (0, lanes - 4 * per)))
    my_rows = lax.dynamic_slice_in_dim(
        upstream_grad, lax.axis_index("fsdp") * rows, rows, 0
    )
    small = jnp.concatenate(
        [joint_bias_grad.reshape(ctx, -1), inner_bias_grad.reshape(ctx, -1), my_rows.reshape(ctx, -1)],
        axis=1,
    ).astype(BF16)
    small = jnp.pad(small[:, None], ((0, 0), (0, 31 - fsdp), (0, lanes - small.shape[1])))
    joint_blocks, dense_blocks = joint_cols // lanes, D // lanes
    terms = jnp.concatenate(
        [
            joint_weight_grad.reshape(fsdp, ctx, per, joint_blocks, lanes)
            .transpose(1, 0, 3, 2, 4).reshape(ctx, -1, lanes),
            dense_weight_grad.reshape(ctx, per, dense_blocks, lanes)
            .transpose(0, 2, 1, 3).reshape(ctx, -1, lanes),
            gains,
            small,
        ],
        axis=1,
    )
    own = ring_reduce(lambda k: lax.dynamic_index_in_dim(terms, k, 0, keepdims=False), "ctx", ctx)
    joint_rows = fsdp * joint_blocks * per
    dense_rows = dense_blocks * per
    ahead = joint_rows + dense_rows
    gain_rows = jnp.pad(own[ahead : ahead + fsdp][:, None], ((0, 0), (0, 15), (0, 0)))
    joint_part = lax.dynamic_slice_in_dim(own, nothing(parts), joint_rows, 0)
    late_rows = joint_blocks * per + 16
    exchanged = jnp.concatenate(
        [
            joint_part.reshape(fsdp, joint_blocks * per, lanes),
            gain_rows,
            ff_own[outer_rows:].reshape(fsdp, per, -1, lanes).transpose(0, 2, 1, 3).reshape(
                fsdp, -1, lanes
            ),
        ],
        axis=1,
    )
    exchanged = lax.all_to_all(exchanged, "fsdp", 0, 0)
    inner_own = exchanged[:, late_rows:].reshape(fsdp, -1, per, lanes).transpose(0, 2, 1, 3)
    ff_own = jnp.concatenate(
        [ff_own[:outer_rows], inner_own.reshape(fsdp * per, inner_cols)], axis=0
    )
    ff_all = lax.all_gather(ff_own, "ctx", axis=0)
    outer_total, inner_total = unpack(ff_all, outer_rows, fsdp)
    gain_own = jnp.sum(exchanged[:, joint_blocks * per].astype(F32), axis=0).astype(BF16)
    own = jnp.concatenate(
        [
            exchanged[:, : joint_blocks * per].reshape(joint_rows, lanes),
            own[joint_rows:ahead],
            jnp.pad(gain_own[None], ((0, fsdp - 1), (0, 0))),
            own[ahead + fsdp :],
        ],
        axis=0,
    )

    def place_late(state, chunk, number, part):
        joint_state, dense_state, vectors = state
        wide = chunk[:joint_rows].reshape(fsdp, joint_blocks, per, lanes).transpose(2, 0, 1, 3)
        joint_state = lax.dynamic_update_slice_in_dim(
            joint_state, wide.reshape(per, -1).astype(F32), number * per, 0
        )
        wide = chunk[joint_rows:ahead].reshape(dense_blocks, per, lanes).transpose(1, 0, 2)
        dense_state = lax.dynamic_update_slice_in_dim(
            dense_state, wide.reshape(per, -1).astype(F32), number * per, 0
        )
        pieces = jnp.stack([chunk[ahead + fsdp], chunk[ahead]])[None]
        vectors = lax.dynamic_update_slice_in_dim(vectors, pieces.astype(F32), number, 0)
        return joint_state, dense_state, vectors

    if per % 16:
        joint_total, dense_total, vectors = ring_gather(
            own, "ctx", ctx, place_late,
            (jnp.zeros(joint_weight.shape, F32), jnp.zeros(dense_weight.shape, F32),
             jnp.zeros((ctx, 2, lanes), F32)),
        )
    else:
        chunks, numbers = ring_gather(
            own, "ctx", ctx,
            lambda state, chunk, number, part: (state[0] + [chunk], state[1] + [number]),
            ([], []),
        )
        joint_total, dense_total, vectors = lay_out(
            jnp.stack(numbers).astype(jnp.int32), chunks, fsdp, joint_blocks, per,
            joint_weight.shape, dense_weight.shape,
        )
        vectors = vectors.reshape(ctx, 16, lanes)
        vectors = jnp.stack([vectors[:, fsdp], vectors[:, 0]], axis=1)
    a, b = joint_cols // ctx, inner_cols // ctx
    joint_bias_total = vectors[:, 0, :a].reshape(-1)
    inner_bias_total = vectors[:, 0, a : a + b].reshape(-1)
    upstream_total = vectors[:, 0, a + b : a + b + per].reshape(-1)
    gain_totals = [vectors[:, 1, k * per : (k + 1) * per].reshape(-1) for k in range(4)]

    layer_output = (tokens[0].astype(F32) + bias_sum
                    + jnp.sum(parts[:, :count].astype(F32), axis=0)).astype(BF16)
    e = jnp.sum(parts[:, count:].astype(F32), axis=0)
    mine = tokens[0].astype(F32)
    mine_centered = mine - jnp.mean(mine, axis=-1, keepdims=True)
    mine_spread = lax.rsqrt(jnp.mean(mine_centered * mine_centered, axis=-1, keepdims=True) + EPSILON)
    mine_normed = mine_centered * mine_spread
    tokens_grad = (
        cotangent[0].astype(F32)
        + (e - jnp.mean(e, axis=-1, keepdims=True)
           - mine_normed * jnp.mean(e * mine_normed, axis=-1, keepdims=True)) * mine_spread
    ).astype(BF16)

    return (
        layer_output[None], tokens_grad[None],
        joint_total, joint_bias_total, dense_total, upstream_total,
        inner_total, inner_bias_total, outer_total, upstream_total,
        gain_totals[0], gain_totals[1], gain_totals[2], gain_totals[3],
    )


def solution(mesh):
    tokens = P("fsdp", "ctx", None)
    weight = P("fsdp", None)
    vector = P("fsdp")
    return jax.shard_map(
        functools.partial(per_device, mesh.shape["ctx"], mesh.shape["fsdp"]),
        mesh=mesh,
        in_specs=(tokens, tokens, P("fsdp", "ctx"), weight) + (weight, vector) * 4 + (vector,) * 4,
        out_specs=(tokens, tokens) + (weight, vector) * 4 + (vector,) * 4,
        check_vma=False,
    )
```

profile of v0, /device:TPU:0, one launch (start us, length us, event | category | flops | bytes accessed | tf_op | source)
XLA Modules:
  0.0 445.7 jit_solution(3932472105689239904)
XLA Ops:
  9.4 3.0 collective-permute-start.2
  12.4 23.1 %collective-permute-done.2 = bf16[2,256,1024]{2,1,0:T(8,128)(2,1)S(1)} collective-permute-done((bf16[2,256,1024]{2,1,0:T(8,128)(2,1)S(1)}, bf16[2,256,1024]{2,1,0:T(8,128)(2,1)S(1)}, u32[]{:S(2)}, u32[]{:S(2)}) %collective-permute-start.2) | collective-permute-done | bytes 1048608 | tf_op jit(solution)/shard_map/ppermute | solution.py:93
  35.8 1.5 pad_maximum_fusion.3
  38.0 1.8 collective-permute-start
  41.1 3.7 all-to-all-start
  46.6 1.9 fusion.30
  48.5 2.4 select_bitcast_fusion.1
  51.4 2.5 copy.55
  53.8 11.0 %all-to-all-done = bf16[4,256,768]{2,1,0:T(8,128)(2,1)S(1)} async-done(((bf16[4,256,768]{2,1,0:T(8,128)(2,1)}), bf16[4,256,768]{2,1,0:T(8,128)(2,1)S(1)}, u32[]{:S(2)}, u32[]{:S(2)}) %all-to-all-start) | async-done | bytes 1572896 | tf_op jit(solution)/shard_map/all_to_all | solution.py:553
  64.8 10.7 %project.1 = (bf16[8,256,512]{2,1,0:T(8,128)(2,1)S(1)}, bf16[1024,1024]{1,0:T(8,128)(2,1)S(1)}, bf16[1024,1024]{1,0:T(8,128)(2,1)S(1)}, bf16[1024,1024]{1,0:T(8,128)(2,1)S(1)}) custom-call(bf16[4,2,256,1024]{3,2,1,0:T(8,128)(2,1)} %bitcast.188, bf16[4,2,256,1024]{3,2,1,0:T(8,128)(2,1)} %bitcast.189, f32[4,1024]{1,0:T(4,128)S(1)} %bitcast.182, ...), custom_call_target="tpu_custom_call" | custom-call | flops 3221225472 | bytes 16777216 | tf_op jit(solution)/shard_map/project/pallas_call | solution.py:166
  76.9 1.4 copy-done.9
  80.9 5.8 %all-to-all-start.1 = ((bf16[8,1,256,512]{3,2,1,0:T(8,128)(2,1)}), bf16[8,1,256,512]{3,2,1,0:T(8,128)(2,1)S(1)}, u32[]{:S(2)}, u32[]{:S(2)}) async-start(bf16[8,1,256,512]{3,2,1,0:T(8,128)(2,1)} %bitcast.177), calls=%async_computation.1 | async-start | bytes 4194304 | tf_op jit(solution)/shard_map/all_to_all | solution.py:515
  86.8 48.0 %all-to-all-done.1 = bf16[8,1,256,512]{3,2,1,0:T(8,128)(2,1)S(1)} async-done(((bf16[8,1,256,512]{3,2,1,0:T(8,128)(2,1)}), bf16[8,1,256,512]{3,2,1,0:T(8,128)(2,1)S(1)}, u32[]{:S(2)}, u32[]{:S(2)}) %all-to-all-start.1) | async-done | bytes 2097184 | tf_op jit(solution)/shard_map/all_to_all | solution.py:515
  137.4 2.8 constant_dynamic-slice_fusion.2
  140.8 1.6 copy-done.8
  142.4 24.9 %attend.1 = bf16[2048,512]{1,0:T(8,128)(2,1)S(1)} custom-call(s32[16]{0:T(128)S(1)} %fusion.51.order_ref, bf16[2048,512]{1,0:T(8,128)(2,1)S(1)} %bitcast.175, bf16[8,256,512]{2,1,0:T(8,128)(2,1)S(1)} %copy-done.8), custom_call_target="tpu_custom_call" | custom-call | flops 30064771072 | bytes 4194304 | tf_op jit(solution)/shard_map/attend/pallas_call | solution.py:347
  169.9 2.0 select_bitcast_fusion.4
  172.9 1.7 fusion.20
  174.6 3.8 all-to-all-start.2
  178.4 3.2 slice.188
  181.7 1.8 select_bitcast_fusion.3
  183.7 1.5 copy.58
  185.2 24.2 %feed.1 = (bf16[1024,1024]{1,0:T(8,128)(2,1)S(1)}, bf16[1024,1024]{1,0:T(8,128)(2,1)S(1)}, f32[1,1024]{1,0:T(1,128)S(1)}, f32[1024,1024]{1,0:T(8,128)}, f32[1024,1024]{1,0:T(8,128)}) custom-call(bf16[1024,1024]{1,0:T(8,128)(2,1)} %copy-done.9, bf16[1024,1024]{1,0:T(8,128)(2,1)} %bitcast.194, bf16[1,1024]{1,0:T(2,128)(2,1)S(1)} %broadcast_in_dim.56.bias_ref, ...), custom_call_target="tpu_custom_call" | custom-call | tf_op jit(solution)/shard_map/feed/pallas_call | solution.py:409
  209.7 2.4 pad_maximum_fusion.1.first_ref
  215.3 2.0 convert_reduce_fusion.2
  217.5 19.8 %all-to-all-done.2 = bf16[8,1,256,512]{3,2,1,0:T(8,128)(2,1)S(1)} async-done(((bf16[8,1,256,512]{3,2,1,0:T(8,128)(2,1)}), bf16[8,1,256,512]{3,2,1,0:T(8,128)(2,1)S(1)}, u32[]{:S(2)}, u32[]{:S(2)}) %all-to-all-start.2) | async-done | bytes 2097184 | tf_op jit(solution)/shard_map/all_to_all | solution.py:596
  237.3 2.2 copy-done
  239.5 2.3 unturn.1
  243.8 1.5 convolution_convert_fusion.1
  245.3 2.4 reshape.369
  247.7 1.9 copy.62
  250.0 5.8 %fusion.2 = (bf16[1024]{0:T(1024)(128)(2,1)S(1)}, bf16[1024]{0:T(1024)(128)(2,1)S(1)}, bf16[1024]{0:T(1024)(128)(2,1)S(1)}, bf16[1024]{0:T(1024)(128)(2,1)S(1)}, bf16[1024,1024]{1,0:T(8,128)(2,1)}) fusion(bf16[1024,1024]{1,0:T(8,128)(2,1)} %copy-done.17, f32[1024,1024]{1,0:T(8,128)} %get-tuple-element.37, f32[1024]{0:T(1024)S(1)} %bitcast.215, ...), kind=kOutput, calls=%fused_computation.8 | convolution fusion | flops 1622142976 | bytes 11550720 | tf_op jit(solution)/shard_map/dot_general | solution.py:26
  256.3 4.6 %convolution_convert_fusion = bf16[1024,768]{1,0:T(8,128)(2,1)} fusion(bf16[1024,1024]{1,0:T(8,128)(2,1)} %copy-done.16, bf16[1024,768]{1,0:T(8,128)(2,1)S(1)} %copy-done.13), kind=kOutput, calls=%fused_computation.31 | convolution fusion | flops 1611399168 | bytes 5242880 | tf_op jit(solution)/shard_map/dot_general | solution.py:26
  260.9 4.4 reshape.367
  265.3 1.5 copy.61
  266.9 3.2 add_convert_fusion.1
  270.1 2.5 pad_maximum_fusion.2
  272.5 5.0 %all-to-all-start.3 = ((bf16[4,512,1024]{2,1,0:T(8,128)(2,1)}), bf16[4,512,1024]{2,1,0:T(8,128)(2,1)}, u32[]{:S(2)}, u32[]{:S(2)}) async-start(bf16[4,512,1024]{2,1,0:T(8,128)(2,1)} %pad_maximum_fusion.2), calls=%async_computation.3 | async-start | bytes 8388608 | tf_op jit(solution)/shard_map/all_to_all | solution.py:602
  277.7 1.6 fusion.5
  279.4 2.0 collective-permute-start.10
  281.5 3.9 collective-permute-done.6
  285.6 1.9 collective-permute-start.7
  288.4 11.6 %collective-permute-done.7 = bf16[544,256]{1,0:T(8,128)(2,1)} collective-permute-done((bf16[544,256]{1,0:T(8,128)(2,1)S(1)}, bf16[544,256]{1,0:T(8,128)(2,1)}, u32[]{:S(2)}, u32[]{:S(2)}) %collective-permute-start.7) | collective-permute-done | bytes 278560 | tf_op jit(solution)/shard_map/ppermute | solution.py:62
  301.0 6.7 %collective-permute-start.8 = (bf16[544,256]{1,0:T(8,128)(2,1)S(1)}, bf16[544,256]{1,0:T(8,128)(2,1)S(1)}, u32[]{:S(2)}, u32[]{:S(2)}) collective-permute-start(bf16[544,256]{1,0:T(8,128)(2,1)S(1)} %bitcast_add_fusion.2), channel_id=1, source_target_pairs={{0,8},{8,16},{16,24},{24,28},{28,20},{20,12},{12,4},{4,0},{1,9},{9... | collective-permute-start | bytes 835592 | tf_op jit(solution)/shard_map/ppermute | solution.py:62
  309.1 4.8 %collective-permute-done.8 = bf16[544,256]{1,0:T(8,128)(2,1)S(1)} collective-permute-done((bf16[544,256]{1,0:T(8,128)(2,1)S(1)}, bf16[544,256]{1,0:T(8,128)(2,1)S(1)}, u32[]{:S(2)}, u32[]{:S(2)}) %collective-permute-start.8) | collective-permute-done | bytes 278560 | tf_op jit(solution)/shard_map/ppermute | solution.py:62
  314.0 3.6 collective-permute-start.12
  318.3 4.1 collective-permute-done.12
  323.2 2.5 collective-permute-start.13
  327.6 2.6 collective-permute-done.13
  330.4 3.3 copy.73
  336.2 11.2 %all_to_all.25 = bf16[4,240,256]{2,1,0:T(8,128)(2,1)S(1)} all-to-all(bf16[4,240,256]{2,1,0:T(8,128)(2,1)S(1)} %fusion.32), channel_id=1, replica_groups=mesh['ctx'=8,'fsdp'=4] {'fsdp'}, dimensions={0} | all-to-all | bytes 983040 | tf_op jit(solution)/shard_map/all_to_all | solution.py:660
  348.9 2.2 collective-permute-start.15
  357.0 2.1 collective-permute-start.17
  360.0 3.7 convert_reduce_fusion
  363.7 14.4 %collective-permute-done.17.refs_4_ = bf16[544,256]{1,0:T(8,128)(2,1)S(1)} collective-permute-done((bf16[544,256]{1,0:T(8,128)(2,1)S(1)}, bf16[544,256]{1,0:T(8,128)(2,1)S(1)}, u32[]{:S(2)}, u32[]{:S(2)}) %collective-permute-start.17) | collective-permute-done | bytes 278560 | tf_op jit(solution)/shard_map/ppermute | solution.py:76
  378.1 2.0 collective-permute-start.18
  380.4 7.0 %collective-permute-done.19.refs_6_ = bf16[544,256]{1,0:T(8,128)(2,1)S(1)} collective-permute-done((bf16[544,256]{1,0:T(8,128)(2,1)S(1)}, bf16[544,256]{1,0:T(8,128)(2,1)S(1)}, u32[]{:S(2)}, u32[]{:S(2)}) %collective-permute-start.19) | collective-permute-done | bytes 278560 | tf_op jit(solution)/shard_map/ppermute | solution.py:76
  387.9 1.6 collective-permute-start.20
  389.6 1.4 fusion.13
  390.9 1.6 collective-permute-done.21
  393.6 2.8 lay_out.1
  400.6 30.7 %all-gather.3.cloned.1.call-done = bf16[2048,1024]{1,0:T(8,128)(2,1)} async-done(((bf16[256,1024]{1,0:T(8,128)(2,1)}), bf16[2048,1024]{1,0:T(8,128)(2,1)}) %all-gather.3.cloned.1.call-update) | async-done | bytes 4194320 | tf_op jit(solution)/shard_map/all_gather | solution.py:665
  431.3 2.2 copy-done.4
  433.5 4.4 unpack.1
  (209 shorter events, 35.1 us)
Async XLA Ops:
  7.2 5.2 %copy-start.30 = (s32[1,256]{1,0:T(1,128)S(1)}, s32[1,256]{1,0:T(1,128)}, u32[]{:S(2)}) copy-start(s32[1,256]{1,0:T(1,128)} %param.20) | copy-start | bytes 3076
  9.4 26.2 %collective-permute-start.2 = (bf16[2,256,1024]{2,1,0:T(8,128)(2,1)S(1)}, bf16[2,256,1024]{2,1,0:T(8,128)(2,1)S(1)}, u32[]{:S(2)}, u32[]{:S(2)}) collective-permute-start(bf16[2,256,1024]{2,1,0:T(8,128)(2,1)S(1)} %constant_dynamic-update-slice_fusion), channel_id=1, source_target_pairs={{0,2},{1,3},{2,0},{3,1},{4,6},{5,7},{6,4},{7,5},{8,10},{9,11},{10,... | collective-permute-start | bytes 3145736 | tf_op jit(solution)/shard_map/ppermute | solution.py:93
  35.7 1.7 copy-start.20
  35.7 2.1 copy-start.21
  35.7 2.1 copy-start.34
  35.7 2.1 copy-start.35
  35.7 2.1 copy-start.36
  35.7 2.1 copy-start.37
  35.7 2.2 copy-start.38
  35.7 2.2 copy-start.39
  35.8 2.2 copy-start.40
  35.8 4.1 copy-start.29
  37.8 10.7 %collective-permute-start.3 = (bf16[2,2,256,1024]{3,2,1,0:T(8,128)(2,1)}, bf16[2,2,256,1024]{3,2,1,0:T(8,128)(2,1)}, u32[]{:S(2)}, u32[]{:S(2)}) collective-permute-start(bf16[2,2,256,1024]{3,2,1,0:T(8,128)(2,1)} %pad_maximum_fusion.3), channel_id=1, source_target_pairs={{0,1},{1,0},{2,3},{3,2},{4,5},{5,4},{6,7},{7,6},{8,9},{9,8},{10,11... | collective-permute-start | bytes 6291464 | tf_op jit(solution)/shard_map/ppermute | solution.py:96
  38.0 6.8 %collective-permute-start = (bf16[16,256]{1,0:T(8,128)(2,1)S(1)}, bf16[16,256]{1,0:T(8,128)(2,1)S(1)}, u32[]{:S(2)}, u32[]{:S(2)}) collective-permute-start(bf16[16,256]{1,0:T(8,128)(2,1)S(1)} %pad.25), channel_id=1, source_target_pairs={{0,2},{1,3},{2,0},{3,1},{4,6},{5,7},{6,4},{7,5},{8,10},{9,11},{10,... | collective-permute-start | bytes 24584 | tf_op jit(solution)/shard_map/ppermute | solution.py:93
  41.1 4.3 copy-start.33
  41.1 23.7 %all-to-all-start = ((bf16[4,256,768]{2,1,0:T(8,128)(2,1)}), bf16[4,256,768]{2,1,0:T(8,128)(2,1)S(1)}, u32[]{:S(2)}, u32[]{:S(2)}) async-start(bf16[4,256,768]{2,1,0:T(8,128)(2,1)} %bitcast.196), calls=%async_computation | async-start | bytes 3145728 | tf_op jit(solution)/shard_map/all_to_all | solution.py:553
  44.8 1.6 collective-permute-start.1
  51.3 13.5 %copy-start.14 = (bf16[256,1024]{1,0:T(8,128)(2,1)S(1)}, bf16[256,1024]{1,0:T(8,128)(2,1)}, u32[]{:S(2)}) copy-start(bf16[256,1024]{1,0:T(8,128)(2,1)} %dense_ref.1) | copy-start | bytes 1572868
  64.8 10.8 %copy-start.10 = (bf16[4,256,768]{2,1,0:T(8,128)(2,1)}, bf16[4,256,768]{2,1,0:T(8,128)(2,1)S(1)}, u32[]{:S(2)}) copy-start(bf16[4,256,768]{2,1,0:T(8,128)(2,1)S(1)} %all-to-all-done) | copy-start | bytes 4718596
  76.9 1.4 copy-start.9
  78.3 1.4 copy-start.16
  80.9 53.9 %all-to-all-start.1 = ((bf16[8,1,256,512]{3,2,1,0:T(8,128)(2,1)}), bf16[8,1,256,512]{3,2,1,0:T(8,128)(2,1)S(1)}, u32[]{:S(2)}, u32[]{:S(2)}) async-start(bf16[8,1,256,512]{3,2,1,0:T(8,128)(2,1)} %bitcast.177), calls=%async_computation.1 | async-start | bytes 4194304 | tf_op jit(solution)/shard_map/all_to_all | solution.py:515
  134.8 1.4 copy-start.2
  137.4 3.4 copy-start.3
  140.1 29.7 %collective-permute-start.4 = (bf16[256,2048]{1,0:T(8,128)(2,1)}, bf16[256,2048]{1,0:T(8,128)(2,1)}, u32[]{:S(2)}, u32[]{:S(2)}) collective-permute-start(bf16[256,2048]{1,0:T(8,128)(2,1)} %constant_dynamic-slice_fusion.2), channel_id=1, source_target_pairs={{0,2},{1,3},{2,0},{3,1},{4,6},{5,7},{6,4},{7,5},{8,10},{9,11},{10,... | collective-permute-start | bytes 3145736 | tf_op jit(solution)/shard_map/ppermute | solution.py:113
  140.8 1.6 copy-start.8
  167.3 1.4 copy-start.1
  171.9 2.6 copy-start.24
  174.6 7.1 %collective-permute-start.5 = (bf16[2,256,1024]{2,1,0:T(8,128)(2,1)}, bf16[2,256,1024]{2,1,0:T(8,128)(2,1)}, u32[]{:S(2)}, u32[]{:S(2)}) collective-permute-start(bf16[2,256,1024]{2,1,0:T(8,128)(2,1)} %fusion.20), channel_id=1, source_target_pairs={{0,1},{1,0},{2,3},{3,2},{4,5},{5,4},{6,7},{7,6},{8,9},{9,8},{10,11... | collective-permute-start | bytes 3145736 | tf_op jit(solution)/shard_map/ppermute | solution.py:117
  174.6 3.8 copy-start.32
  174.6 62.7 %all-to-all-start.2 = ((bf16[8,1,256,512]{3,2,1,0:T(8,128)(2,1)}), bf16[8,1,256,512]{3,2,1,0:T(8,128)(2,1)S(1)}, u32[]{:S(2)}, u32[]{:S(2)}) async-start(bf16[8,1,256,512]{3,2,1,0:T(8,128)(2,1)} %bitcast.173), calls=%async_computation.2 | async-start | bytes 4194304 | tf_op jit(solution)/shard_map/all_to_all | solution.py:596
  178.3 156.6 %reduce-scatter.2.cloned.1.call-start = ((), (), s32[]{:S(2)}) async-start(), calls=%async_computation.6 | async-start | bytes 4718592 | tf_op jit(solution)/shard_map/reduce_scatter | solution.py:595
  178.4 3.2 copy-start.23
  178.4 3.2 copy-start.25
  237.3 2.2 copy-start
  239.5 4.3 copy-start.18
  243.8 5.9 %copy-start.13 = (bf16[1024,768]{1,0:T(8,128)(2,1)S(1)}, bf16[1024,768]{1,0:T(8,128)(2,1)}, u32[]{:S(2)}) copy-start(bf16[1024,768]{1,0:T(8,128)(2,1)} %copy-done.12) | copy-start | bytes 4718596
  245.3 4.7 %copy-start.11 = (bf16[4,256,768]{2,1,0:T(8,128)(2,1)S(1)}, bf16[4,256,768]{2,1,0:T(8,128)(2,1)}, u32[]{:S(2)}) copy-start(bf16[4,256,768]{2,1,0:T(8,128)(2,1)} %copy-done.10) | copy-start | bytes 4718596
  265.3 1.6 copy-start.6
  265.3 1.5 copy-start.15
  266.9 3.2 copy-start.27
  272.5 5.2 %copy-start.26 = (bf16[8,32,4,256]{3,1,2,0:T(8,128)(2,1)S(1)}, bf16[8,32,4,256]{3,1,2,0:T(8,128)(2,1)}, u32[]{:S(2)}) copy-start(bf16[8,32,4,256]{3,1,2,0:T(8,128)(2,1)} %copy.62) | copy-start | bytes 1572868
  272.5 57.8 %all-to-all-start.3 = ((bf16[4,512,1024]{2,1,0:T(8,128)(2,1)}), bf16[4,512,1024]{2,1,0:T(8,128)(2,1)}, u32[]{:S(2)}, u32[]{:S(2)}) async-start(bf16[4,512,1024]{2,1,0:T(8,128)(2,1)} %pad_maximum_fusion.2), calls=%async_computation.3 | async-start | bytes 8388608 | tf_op jit(solution)/shard_map/all_to_all | solution.py:602
  277.5 153.8 %all-gather.3.cloned.1.call-start = ((), (), s32[]{:S(2)}) async-start(), calls=%async_computation.7 | async-start | bytes 4718592 | tf_op jit(solution)/shard_map/all_gather | solution.py:665
  279.4 6.0 %collective-permute-start.6 = (bf16[272,256]{1,0:T(8,128)(2,1)S(1)}, bf16[272,256]{1,0:T(8,128)(2,1)S(1)}, u32[]{:S(2)}, u32[]{:S(2)}) collective-permute-start(bf16[272,256]{1,0:T(8,128)(2,1)S(1)} %get-tuple-element.73), channel_id=1, source_target_pairs={{0,8},{8,16},{16,24},{24,28},{28,20},{20,12},{12,4},{4,0},{1,9},{9... | collective-permute-start | bytes 417800 | tf_op jit(solution)/shard_map/ppermute | solution.py:51
  279.4 6.0 %collective-permute-start.10 = (bf16[272,256]{1,0:T(8,128)(2,1)S(1)}, bf16[272,256]{1,0:T(8,128)(2,1)S(1)}, u32[]{:S(2)}, u32[]{:S(2)}) collective-permute-start(bf16[272,256]{1,0:T(8,128)(2,1)S(1)} %get-tuple-element.75), channel_id=1, source_target_pairs={{8,0},{16,8},{24,16},{28,24},{20,28},{12,20},{4,12},{0,4},{9,1},{1... | collective-permute-start | bytes 417800 | tf_op jit(solution)/shard_map/ppermute | solution.py:52
  285.6 14.5 %collective-permute-start.7 = (bf16[544,256]{1,0:T(8,128)(2,1)S(1)}, bf16[544,256]{1,0:T(8,128)(2,1)}, u32[]{:S(2)}, u32[]{:S(2)}) collective-permute-start(bf16[544,256]{1,0:T(8,128)(2,1)S(1)} %pad_maximum_fusion.6), channel_id=1, source_target_pairs={{0,8},{8,16},{16,24},{24,28},{28,20},{20,12},{12,4},{4,0},{1,9},{9... | collective-permute-start | bytes 835592 | tf_op jit(solution)/shard_map/ppermute | solution.py:62
  288.2 20.9 %collective-permute-start.11 = (bf16[544,256]{1,0:T(8,128)(2,1)S(1)}, bf16[544,256]{1,0:T(8,128)(2,1)S(1)}, u32[]{:S(2)}, u32[]{:S(2)}) collective-permute-start(bf16[544,256]{1,0:T(8,128)(2,1)S(1)} %pad_maximum_fusion.7), channel_id=1, source_target_pairs={{8,0},{16,8},{24,16},{28,24},{20,28},{12,20},{4,12},{0,4},{9,1},{1... | collective-permute-start | bytes 835592 | tf_op jit(solution)/shard_map/ppermute | solution.py:63
  301.0 12.9 %collective-permute-start.8 = (bf16[544,256]{1,0:T(8,128)(2,1)S(1)}, bf16[544,256]{1,0:T(8,128)(2,1)S(1)}, u32[]{:S(2)}, u32[]{:S(2)}) collective-permute-start(bf16[544,256]{1,0:T(8,128)(2,1)S(1)} %bitcast_add_fusion.2), channel_id=1, source_target_pairs={{0,8},{8,16},{16,24},{24,28},{28,20},{20,12},{12,4},{4,0},{1,9},{9... | collective-permute-start | bytes 835592 | tf_op jit(solution)/shard_map/ppermute | solution.py:62
  314.0 8.5 %collective-permute-start.12 = (bf16[544,256]{1,0:T(8,128)(2,1)S(1)}, bf16[544,256]{1,0:T(8,128)(2,1)S(1)}, u32[]{:S(2)}, u32[]{:S(2)}) collective-permute-start(bf16[544,256]{1,0:T(8,128)(2,1)S(1)} %get-tuple-element.70), channel_id=1, source_target_pairs={{8,0},{16,8},{24,16},{28,24},{20,28},{12,20},{4,12},{0,4},{9,1},{1... | collective-permute-start | bytes 835592 | tf_op jit(solution)/shard_map/ppermute | solution.py:63
  318.3 9.3 %collective-permute-start.9 = (bf16[544,256]{1,0:T(8,128)(2,1)S(1)}, bf16[544,256]{1,0:T(8,128)(2,1)S(1)}, u32[]{:S(2)}, u32[]{:S(2)}) collective-permute-start(bf16[544,256]{1,0:T(8,128)(2,1)S(1)} %get-tuple-element.69), channel_id=1, source_target_pairs={{0,8},{8,16},{16,24},{24,28},{28,20},{20,12},{12,4},{4,0},{1,9},{9... | collective-permute-start | bytes 835592 | tf_op jit(solution)/shard_map/ppermute | solution.py:62
  323.2 7.1 %collective-permute-start.13 = (bf16[544,256]{1,0:T(8,128)(2,1)}, bf16[544,256]{1,0:T(8,128)(2,1)S(1)}, u32[]{:S(2)}, u32[]{:S(2)}) collective-permute-start(bf16[544,256]{1,0:T(8,128)(2,1)} %bitcast_add_fusion.1), channel_id=1, source_target_pairs={{8,0},{16,8},{24,16},{28,24},{20,28},{12,20},{4,12},{0,4},{9,1},{1... | collective-permute-start | bytes 835592 | tf_op jit(solution)/shard_map/ppermute | solution.py:63
  336.2 12.3 %copy-start.19 = (bf16[1,256,1024]{2,1,0:T(8,128)(2,1)S(1)}, bf16[1,256,1024]{2,1,0:T(8,128)(2,1)}, u32[]{:S(2)}) copy-start(bf16[1,256,1024]{2,1,0:T(8,128)(2,1)} %param.18) | copy-start | bytes 1572868
  348.9 8.2 %collective-permute-start.15 = (bf16[544,256]{1,0:T(8,128)(2,1)S(1)}, bf16[544,256]{1,0:T(8,128)(2,1)S(1)}, u32[]{:S(2)}, u32[]{:S(2)}) collective-permute-start(bf16[544,256]{1,0:T(8,128)(2,1)S(1)} %fusion.34.refs_0_), channel_id=1, source_target_pairs={{8,0},{16,8},{24,16},{28,24},{20,28},{12,20},{4,12},{0,4},{9,1},{1... | collective-permute-start | bytes 835592 | tf_op jit(solution)/shard_map/ppermute | solution.py:76
  351.0 8.9 %collective-permute-start.14 = (bf16[544,256]{1,0:T(8,128)(2,1)S(1)}, bf16[544,256]{1,0:T(8,128)(2,1)S(1)}, u32[]{:S(2)}, u32[]{:S(2)}) collective-permute-start(bf16[544,256]{1,0:T(8,128)(2,1)S(1)} %fusion.34.refs_0_), channel_id=1, source_target_pairs={{0,8},{8,16},{16,24},{24,28},{28,20},{20,12},{12,4},{4,0},{1,9},{9... | collective-permute-start | bytes 835592 | tf_op jit(solution)/shard_map/ppermute | solution.py:75
  357.0 21.0 %collective-permute-start.17 = (bf16[544,256]{1,0:T(8,128)(2,1)S(1)}, bf16[544,256]{1,0:T(8,128)(2,1)S(1)}, u32[]{:S(2)}, u32[]{:S(2)}) collective-permute-start(bf16[544,256]{1,0:T(8,128)(2,1)S(1)} %collective-permute-done.15.refs_2_), channel_id=1, source_target_pairs={{8,0},{16,8},{24,16},{28,24},{20,28},{12,20},{4,12},{0,4},{9,1},{1... | collective-permute-start | bytes 835592 | tf_op jit(solution)/shard_map/ppermute | solution.py:76
  360.0 18.1 %collective-permute-start.16 = (bf16[544,256]{1,0:T(8,128)(2,1)S(1)}, bf16[544,256]{1,0:T(8,128)(2,1)S(1)}, u32[]{:S(2)}, u32[]{:S(2)}) collective-permute-start(bf16[544,256]{1,0:T(8,128)(2,1)S(1)} %collective-permute-done.14.refs_1_), channel_id=1, source_target_pairs={{0,8},{8,16},{16,24},{24,28},{28,20},{20,12},{12,4},{4,0},{1,9},{9... | collective-permute-start | bytes 835592 | tf_op jit(solution)/shard_map/ppermute | solution.py:75
  363.6 25.9 %copy-start.28 = (bf16[1,256,1024]{2,1,0:T(8,128)(2,1)S(1)}, bf16[1,256,1024]{2,1,0:T(8,128)(2,1)}, u32[]{:S(2)}) copy-start(bf16[1,256,1024]{2,1,0:T(8,128)(2,1)} %param.19) | copy-start | bytes 1572868
  378.1 9.4 %collective-permute-start.19 = (bf16[544,256]{1,0:T(8,128)(2,1)S(1)}, bf16[544,256]{1,0:T(8,128)(2,1)S(1)}, u32[]{:S(2)}, u32[]{:S(2)}) collective-permute-start(bf16[544,256]{1,0:T(8,128)(2,1)S(1)} %collective-permute-done.17.refs_4_), channel_id=1, source_target_pairs={{8,0},{16,8},{24,16},{28,24},{20,28},{12,20},{4,12},{0,4},{9,1},{1... | collective-permute-start | bytes 835592 | tf_op jit(solution)/shard_map/ppermute | solution.py:76
  378.1 9.8 %collective-permute-start.18 = (bf16[544,256]{1,0:T(8,128)(2,1)S(1)}, bf16[544,256]{1,0:T(8,128)(2,1)S(1)}, u32[]{:S(2)}, u32[]{:S(2)}) collective-permute-start(bf16[544,256]{1,0:T(8,128)(2,1)S(1)} %collective-permute-done.16.refs_3_), channel_id=1, source_target_pairs={{0,8},{8,16},{16,24},{24,28},{28,20},{20,12},{12,4},{4,0},{1,9},{9... | collective-permute-start | bytes 835592 | tf_op jit(solution)/shard_map/ppermute | solution.py:75
  387.4 5.1 %collective-permute-start.21 = (bf16[272,256]{1,0:T(8,128)(2,1)S(1)}, bf16[272,256]{1,0:T(8,128)(2,1)S(1)}, u32[]{:S(2)}, u32[]{:S(2)}) collective-permute-start(bf16[272,256]{1,0:T(8,128)(2,1)S(1)} %dynamic_slice.84), channel_id=1, source_target_pairs={{8,0},{16,8},{24,16},{28,24},{20,28},{12,20},{4,12},{0,4},{9,1},{1... | collective-permute-start | bytes 417800 | tf_op jit(solution)/shard_map/ppermute | solution.py:80
  387.9 5.7 %collective-permute-start.20 = (bf16[272,256]{1,0:T(8,128)(2,1)S(1)}, bf16[272,256]{1,0:T(8,128)(2,1)S(1)}, u32[]{:S(2)}, u32[]{:S(2)}) collective-permute-start(bf16[272,256]{1,0:T(8,128)(2,1)S(1)} %dynamic_slice.83), channel_id=1, source_target_pairs={{0,8},{8,16},{16,24},{24,28},{28,20},{20,12},{12,4},{4,0},{1,9},{9... | collective-permute-start | bytes 417800 | tf_op jit(solution)/shard_map/ppermute | solution.py:79
  398.7 39.2 %copy-start.31 = (f32[256]{0:T(256)}, f32[256]{0:T(256)S(1)}, u32[]{:S(2)}) copy-start(f32[256]{0:T(256)S(1)} %reshape_squeeze.31) | copy-start | bytes 3076
  431.3 2.2 copy-start.4
  (6 other events, 6.2 us)
Sparse Core Ops, SparseCore 0:
  212.2 99.0 reduce-scatter.1
  348.7 82.5 all-gather.2
where the time goes:
time: 454 us; the launch traced here: 446 us
  waiting for transfers between devices  186 us (41%)
  Pallas kernels  69.4 us (15%)
  local copies, waits for them, and re-layouts  55.4 us (12%)
  starting transfers between devices  49.9 us (11%)
  other arithmetic  29.8 us (7%)
  between operations  28.6 us (6%)
  matrix products  15.1 us (3%)
  blocking collectives  11.2 us (2%)
    all_to_all x1, waiting for transfers between devices, spread_out(): lax.all_to_all(part.reshape((ctx, each) + part.shape[1:]), 'ctx', 0, 0)  48 us
    all_gather x1, waiting for transfers between devices, per_device(): ff_all = lax.all_gather(ff_own, 'ctx', axis=0)  30.7 us
    pallas_call x1, Pallas kernels, attend(): pl.pallas_call(functools.partial(attend_kernel, tile, block, unrolled), g...  24.9 us
    pallas_call x1, Pallas kernels, feed(): pl.pallas_call(feed_kernel, grid=(columns // tile,), in_specs=[whole, pl....  24.2 us
    unnamed x91, local copies, waits for them, and re-layouts  23.2 us
    ppermute x2, waiting for transfers between devices, gather_pairs(): across = lax.ppermute(own, 'fsdp', [(k, k ^ 2) for k in range(4)])  23.1 us
    ppermute x3, waiting for transfers between devices, ring_gather(): down = lax.ppermute(down, axis, back)  21.7 us
    all_to_all x1, waiting for transfers between devices, per_device(): lax.all_to_all(back, 'ctx', 0, 0)[:jobs // each]  19.8 us
  transfers between devices with their start and end apart: 28, of which 18 were waited for; matrix products, arithmetic and copies ran while one was open for 16% of the time, Pallas kernels for 12%

commit v1 on v0

--- a/solution.py
+++ b/solution.py
@@ -509,6 +509,39 @@
     )(numbers, *chunks)
 
 
+def lay_out_wide_kernel(outer_rows, parts, numbers_ref, *refs):
+    count = len(refs) - 2
+    outer_ref, inner_ref = refs[count:]
+    width = outer_ref.shape[1]
+    per = inner_ref.shape[0] // count
+    for k in range(count):
+        start = pl.multiple_of(numbers_ref[k] * outer_rows, outer_rows)
+        outer_ref[pl.ds(start, outer_rows), :] = refs[k][:outer_rows].astype(F32)
+        rows = pl.ds(pl.multiple_of(numbers_ref[k] * per, per), per)
+        for part in range(parts):
+            first = outer_rows + part * per
+            inner_ref[rows, part * width : (part + 1) * width] = refs[k][first : first + per].astype(F32)
+
+
+def lay_out_wide(numbers, chunks, outer_rows, parts):
+    rows, width = chunks[0].shape
+    count = len(chunks)
+    per = (rows - outer_rows) // parts
+    whole = pl.BlockSpec(memory_space=pltpu.VMEM)
+    return pl.pallas_call(
+        functools.partial(lay_out_wide_kernel, outer_rows, parts),
+        in_specs=[pl.BlockSpec(memory_space=pltpu.SMEM)] + [whole] * count,
+        out_specs=[whole] * 2,
+        out_shape=[
+            jax.ShapeDtypeStruct((count * outer_rows, width), F32),
+            jax.ShapeDtypeStruct((count * per, parts * width), F32),
+        ],
+        compiler_params=pltpu.CompilerParams(vmem_limit_bytes=24 * MIB),
+        cost_estimate=pl.CostEstimate(flops=0, bytes_accessed=12 * MIB, transcendentals=0),
+        name="lay_out_wide",
+    )(numbers, *chunks)
+
+
 def spread_out(part, ctx, each):
     if ctx > part.shape[0]:
         part = jnp.concatenate([part] * (ctx // part.shape[0]), axis=0)
@@ -592,7 +625,9 @@
         ],
         axis=1,
     )
-    ff_own = lax.psum_scatter(ff_terms, "ctx", scatter_dimension=0)
+    ff_own = ring_reduce(
+        lambda k: lax.dynamic_index_in_dim(ff_terms, k, 0, keepdims=False), "ctx", ctx
+    )
     back = lax.all_to_all(back, "ctx", 0, 0)[: jobs // each].reshape(jobs, count, 4 * PAIR)
     joint_grad, mixed = unturn(back, cosine, sine, ff_terms, seqs, count, pairs)
 
@@ -662,8 +697,18 @@
     ff_own = jnp.concatenate(
         [ff_own[:outer_rows], inner_own.reshape(fsdp * per, inner_cols)], axis=0
     )
-    ff_all = lax.all_gather(ff_own, "ctx", axis=0)
-    outer_total, inner_total = unpack(ff_all, outer_rows, fsdp)
+    if per % 16:
+        ff_all = lax.all_gather(ff_own, "ctx", axis=0)
+        outer_total, inner_total = unpack(ff_all, outer_rows, fsdp)
+    else:
+        ff_chunks, ff_numbers = ring_gather(
+            ff_own, "ctx", ctx,
+            lambda state, chunk, number, part: (state[0] + [chunk], state[1] + [number]),
+            ([], []),
+        )
+        outer_total, inner_total = lay_out_wide(
+            jnp.stack(ff_numbers).astype(jnp.int32), ff_chunks, outer_rows, fsdp
+        )
     gain_own = jnp.sum(exchanged[:, joint_blocks * per].astype(F32), axis=0).astype(BF16)
     own = jnp.concatenate(
         [

time: 454 us -> 434 us (0.956)
  waiting for transfers between devices: 186 us -> 159 us
  other arithmetic: 29.8 us -> 45.5 us
  between operations: 28.6 us -> 15.4 us
  starting transfers between devices: 49.9 us -> 62.5 us
  blocking collectives: 11.2 us -> 0 us
    all_gather x1 -> x0, waiting for transfers between devices: 30.7 us -> none  [per_device(): ff_all = lax.all_gather(ff_own, 'ctx', axis=0)]
    all_to_all x1, waiting for transfers between devices: 19.8 us -> 0.01 us  [per_device(): lax.all_to_all(back, 'ctx', 0, 0)[:jobs // each]]
    all_to_all x1 -> x0, blocking collectives: 11.2 us -> none  [per_device(): exchanged = lax.all_to_all(exchanged, 'fsdp', 0, 0)]
    ppermute x3 -> x6, waiting for transfers between devices: 21.7 us -> 30.7 us  [ring_gather(): down = lax.ppermute(down, axis, back)]
    all_to_all x0 -> x1, waiting for transfers between devices: none -> 8.26 us  [per_device(): exchanged = lax.all_to_all(exchanged, 'fsdp', 0, 0)]
    add x2 -> x4, other arithmetic: 1.05 us -> 9.11 us  [ring_reduce(): mine_up = mine_up + up]
    ppermute x1 -> x2, waiting for transfers between devices: 0.07 us -> 7.61 us  [ring_reduce(): down = lax.ppermute(far[rows:], axis, back)]
    ppermute x3 -> x6, waiting for transfers between devices: 6.7 us -> 11.8 us  [ring_reduce(): down = lax.ppermute(mine_down, axis, back)]
  transfers between devices with their start and end apart: 28 -> 43, of which waited for: 18 -> 15; matrix products, arithmetic and copies ran while one was open for 16% -> 21% of each run, Pallas kernels for 12% -> 14%
where the time goes in v1:
time: 434 us; the launch traced here: 427 us
  waiting for transfers between devices  159 us (37%)
  Pallas kernels  73.8 us (17%)
  starting transfers between devices  62.5 us (14%)
  local copies, waits for them, and re-layouts  56 us (13%)
  other arithmetic  45.5 us (10%)
  between operations  15.4 us (4%)
  matrix products  15.2 us (4%)
    all_to_all x1, waiting for transfers between devices, spread_out(): lax.all_to_all(part.reshape((ctx, each) + part.shape[1:]), 'ctx', 0, 0)  48 us
    ppermute x6, waiting for transfers between devices, ring_gather(): down = lax.ppermute(down, axis, back)  30.7 us
    pallas_call x1, Pallas kernels, attend(): pl.pallas_call(functools.partial(attend_kernel, tile, block, unrolled), g...  26.5 us
    pallas_call x1, Pallas kernels, feed(): pl.pallas_call(feed_kernel, grid=(columns // tile,), in_specs=[whole, pl....  24 us
    ppermute x2, waiting for transfers between devices, gather_pairs(): across = lax.ppermute(own, 'fsdp', [(k, k ^ 2) for k in range(4)])  23.1 us
    unnamed x99, local copies, waits for them, and re-layouts  22.7 us
    ppermute x6, waiting for transfers between devices, ring_reduce(): up = lax.ppermute(mine_up, axis, onward)  17.2 us
    dot_general x4, matrix products, dot(): lax.dot_general(left, right, (((left_dim,), (right_dim,)), ((), ())), pre...  15.2 us
  transfers between devices with their start and end apart: 43, of which 15 were waited for; matrix products, arithmetic and copies ran while one was open for 21% of the time, Pallas kernels for 14%

profile of v1, /device:TPU:0, one launch (start us, length us, event | category | flops | bytes accessed | tf_op | source)
XLA Modules:
  0.0 427.2 jit_solution(1627976611015498095)
XLA Ops:
  2.8 3.0 collective-permute-start.2
  5.8 23.1 %collective-permute-done.2 = bf16[2,256,1024]{2,1,0:T(8,128)(2,1)S(1)} collective-permute-done((bf16[2,256,1024]{2,1,0:T(8,128)(2,1)S(1)}, bf16[2,256,1024]{2,1,0:T(8,128)(2,1)S(1)}, u32[]{:S(2)}, u32[]{:S(2)}) %collective-permute-start.2) | collective-permute-done | bytes 1048608 | tf_op jit(solution)/shard_map/ppermute | solution.py:93
  29.2 1.5 pad_maximum_fusion.3
  31.5 1.8 collective-permute-start
  34.5 3.7 all-to-all-start
  40.0 1.9 fusion.40
  42.0 2.4 select_bitcast_fusion.1
  44.8 2.5 copy.55
  47.3 11.0 %all-to-all-done = bf16[4,256,768]{2,1,0:T(8,128)(2,1)S(1)} async-done(((bf16[4,256,768]{2,1,0:T(8,128)(2,1)}), bf16[4,256,768]{2,1,0:T(8,128)(2,1)S(1)}, u32[]{:S(2)}, u32[]{:S(2)}) %all-to-all-start) | async-done | bytes 1572896 | tf_op jit(solution)/shard_map/all_to_all | solution.py:586
  58.3 10.7 %project.1 = (bf16[8,256,512]{2,1,0:T(8,128)(2,1)S(1)}, bf16[1024,1024]{1,0:T(8,128)(2,1)S(1)}, bf16[1024,1024]{1,0:T(8,128)(2,1)S(1)}, bf16[1024,1024]{1,0:T(8,128)(2,1)S(1)}) custom-call(bf16[4,2,256,1024]{3,2,1,0:T(8,128)(2,1)} %bitcast.219, bf16[4,2,256,1024]{3,2,1,0:T(8,128)(2,1)} %bitcast.220, f32[4,1024]{1,0:T(4,128)S(1)} %bitcast.208, ...), custom_call_target="tpu_custom_call" | custom-call | flops 3221225472 | bytes 16777216 | tf_op jit(solution)/shard_map/project/pallas_call | solution.py:166
  74.4 5.8 %all-to-all-start.1 = ((bf16[8,1,256,512]{3,2,1,0:T(8,128)(2,1)}), bf16[8,1,256,512]{3,2,1,0:T(8,128)(2,1)S(1)}, u32[]{:S(2)}, u32[]{:S(2)}) async-start(bf16[8,1,256,512]{3,2,1,0:T(8,128)(2,1)} %bitcast.204), calls=%async_computation.1 | async-start | bytes 4194304 | tf_op jit(solution)/shard_map/all_to_all | solution.py:548
  80.2 48.0 %all-to-all-done.1 = bf16[8,1,256,512]{3,2,1,0:T(8,128)(2,1)S(1)} async-done(((bf16[8,1,256,512]{3,2,1,0:T(8,128)(2,1)}), bf16[8,1,256,512]{3,2,1,0:T(8,128)(2,1)S(1)}, u32[]{:S(2)}, u32[]{:S(2)}) %all-to-all-start.1) | async-done | bytes 2097184 | tf_op jit(solution)/shard_map/all_to_all | solution.py:548
  130.5 2.8 constant_dynamic-slice_fusion.2
  133.9 26.5 %attend.1 = bf16[2048,512]{1,0:T(8,128)(2,1)} custom-call(s32[16]{0:T(128)S(1)} %fusion.63.order_ref, bf16[2048,512]{1,0:T(8,128)(2,1)S(1)} %bitcast.203, bf16[8,256,512]{2,1,0:T(8,128)(2,1)S(1)} %copy-done.4), custom_call_target="tpu_custom_call" | custom-call | flops 30064771072 | bytes 4194304 | tf_op jit(solution)/shard_map/attend/pallas_call | solution.py:347
  160.4 2.7 copy.72
  164.3 4.5 %all-to-all-start.2 = ((bf16[8,1,256,512]{3,2,1,0:T(8,128)(2,1)}), bf16[8,1,256,512]{3,2,1,0:T(8,128)(2,1)}, u32[]{:S(2)}, u32[]{:S(2)}) async-start(bf16[8,1,256,512]{3,2,1,0:T(8,128)(2,1)} %bitcast.32), calls=%async_computation.2 | async-start | bytes 4194304 | tf_op jit(solution)/shard_map/all_to_all | solution.py:631
  168.8 2.0 select_bitcast_fusion.4
  170.9 1.7 fusion.20
  176.6 3.2 slice.231
  180.3 1.8 select_bitcast_fusion.3
  182.3 1.5 copy.58
  183.8 24.0 %feed.1 = (bf16[1024,1024]{1,0:T(8,128)(2,1)S(1)}, bf16[1024,1024]{1,0:T(8,128)(2,1)S(1)}, f32[1,1024]{1,0:T(1,128)S(1)}, f32[1024,1024]{1,0:T(8,128)}, f32[1024,1024]{1,0:T(8,128)}) custom-call(bf16[1024,1024]{1,0:T(8,128)(2,1)} %copy-done.5, bf16[1024,1024]{1,0:T(8,128)(2,1)} %bitcast.225, bf16[1,1024]{1,0:T(2,128)(2,1)S(1)} %broadcast_in_dim.56.bias_ref, ...), custom_call_target="tpu_custom_call" | custom-call | tf_op jit(solution)/shard_map/feed/pallas_call | solution.py:409
  208.3 1.9 collective-permute-start.18
  210.3 2.7 pad_maximum_fusion.first_ref
  214.1 7.6 %collective-permute-done.18 = bf16[128,1024]{1,0:T(8,128)(2,1)S(1)} collective-permute-done((bf16[128,1024]{1,0:T(8,128)(2,1)S(1)}, bf16[128,1024]{1,0:T(8,128)(2,1)S(1)}, u32[]{:S(2)}, u32[]{:S(2)}) %collective-permute-start.18) | collective-permute-done | bytes 262176 | tf_op jit(solution)/shard_map/ppermute | solution.py:52
  223.4 2.2 collective-permute-start.15
  225.6 2.2 copy-done
  227.8 5.3 %unturn.1 = (bf16[1024,768]{1,0:T(8,128)(2,1)S(1)}, bf16[1024,256]{1,0:T(8,128)(2,1)S(1)}) custom-call(bf16[8,256,512]{2,1,0:T(8,128)(2,1)} %bitcast.33.back_ref, f32[1024,128]{1,0:T(8,128)S(1)} %get-tuple-element.103.cos_ref, f32[1024,128]{1,0:T(8,128)S(1)} %get-tuple-element.102.sin_ref, bf16[8,256,1024]{2,1,0:T(8,128)(2,1)S(1)} %copy-done), custom_call_target="tpu_custom_call" | custom-call | flops 8388608 | bytes 5242880 | tf_op jit(solution)/shard_map/unturn/pallas_call | solution.py:212
  235.1 1.7 reduce.5
  236.8 5.3 %convolution_convert_fusion = bf16[1024,768]{1,0:T(8,128)(2,1)} fusion(bf16[1024,1024]{1,0:T(8,128)(2,1)} %copy-done.19, bf16[1024,768]{1,0:T(8,128)(2,1)} %copy-done.7), kind=kOutput, calls=%fused_computation.47 | convolution fusion | flops 1611399168 | bytes 5242880 | tf_op jit(solution)/shard_map/dot_general | solution.py:26
  242.1 1.5 convolution_convert_fusion.1
  246.0 7.6 %fusion.2 = (bf16[1024]{0:T(1024)(128)(2,1)S(1)}, bf16[1024]{0:T(1024)(128)(2,1)S(1)}, bf16[1024]{0:T(1024)(128)(2,1)S(1)}, bf16[1024]{0:T(1024)(128)(2,1)S(1)}, bf16[1024,1024]{1,0:T(8,128)(2,1)}) fusion(bf16[1024,1024]{1,0:T(8,128)(2,1)} %copy-done.18, f32[1024,1024]{1,0:T(8,128)} %get-tuple-element.37, f32[1024]{0:T(1024)S(1)} %bitcast.244, ...), kind=kOutput, calls=%fused_computation.25 | convolution fusion | flops 1622142976 | bytes 11550720 | tf_op jit(solution)/shard_map/dot_general | solution.py:26
  254.1 5.3 %reshape.386 = bf16[4,8,32,3,256]{4,3,2,1,0:T(4,128)(2,1)} reshape(bf16[1024,768]{1,0:T(8,128)(2,1)} %convolution_convert_fusion) | data formatting | bytes 3145728 | tf_op jit(solution)/shard_map/reshape | solution.py:669
  259.3 2.0 copy.61
  267.7 2.5 pad_maximum_fusion.2
  270.2 4.9 %all-to-all-start.3 = ((bf16[4,512,1024]{2,1,0:T(8,128)(2,1)}), bf16[4,512,1024]{2,1,0:T(8,128)(2,1)}, u32[]{:S(2)}, u32[]{:S(2)}) async-start(bf16[4,512,1024]{2,1,0:T(8,128)(2,1)} %pad_maximum_fusion.2), calls=%async_computation.3 | async-start | bytes 8388608 | tf_op jit(solution)/shard_map/all_to_all | solution.py:637
  275.1 2.8 bitcast_add_fusion.2
  285.2 13.2 %collective-permute-done.7 = bf16[544,256]{1,0:T(8,128)(2,1)} collective-permute-done((bf16[544,256]{1,0:T(8,128)(2,1)}, bf16[544,256]{1,0:T(8,128)(2,1)}, u32[]{:S(2)}, u32[]{:S(2)}) %collective-permute-start.7) | collective-permute-done | bytes 278560 | tf_op jit(solution)/shard_map/ppermute | solution.py:62
  298.4 1.8 bitcast_add_fusion.6
  301.5 2.6 bitcast_add_fusion.3
  304.6 1.5 collective-permute-start.21
  306.1 4.0 collective-permute-done.8
  310.1 2.0 bitcast_add_fusion.7
  314.0 2.1 collective-permute-start.9
  316.1 7.7 %collective-permute-done.12 = bf16[544,256]{1,0:T(8,128)(2,1)} collective-permute-done((bf16[544,256]{1,0:T(8,128)(2,1)}, bf16[544,256]{1,0:T(8,128)(2,1)}, u32[]{:S(2)}, u32[]{:S(2)}) %collective-permute-start.12) | collective-permute-done | bytes 278560 | tf_op jit(solution)/shard_map/ppermute | solution.py:63
  323.8 1.8 bitcast_add_fusion.5
  325.6 1.7 collective-permute-start.13
  328.8 4.1 collective-permute-done.13
  334.1 3.3 copy.73
  339.5 3.5 all-to-all-start.4
  343.2 8.3 %all-to-all-done.4 = bf16[4,240,256]{2,1,0:T(8,128)(2,1)S(1)} async-done(((bf16[4,240,256]{2,1,0:T(8,128)(2,1)}), bf16[4,240,256]{2,1,0:T(8,128)(2,1)S(1)}, u32[]{:S(2)}, u32[]{:S(2)}) %all-to-all-start.4) | async-done | bytes 491552 | tf_op jit(solution)/shard_map/all_to_all | solution.py:695
  351.7 1.5 collective-permute-start.31
  353.9 1.5 collective-permute-start.23
  362.2 9.1 %collective-permute-done.23.refs_2_ = bf16[544,256]{1,0:T(8,128)(2,1)S(1)} collective-permute-done((bf16[544,256]{1,0:T(8,128)(2,1)S(1)}, bf16[544,256]{1,0:T(8,128)(2,1)S(1)}, u32[]{:S(2)}, u32[]{:S(2)}) %collective-permute-start.23) | collective-permute-done | bytes 278560 | tf_op jit(solution)/shard_map/ppermute | solution.py:76
  373.3 1.5 collective-permute-start.33
  375.3 3.7 convert_reduce_fusion
  379.0 1.8 collective-permute-done.25.refs_4_
  380.8 1.5 collective-permute-start.27
  383.2 8.9 %collective-permute-done.33.refs_4_ = bf16[256,1024]{1,0:T(8,128)(2,1)S(1)} collective-permute-done((bf16[256,1024]{1,0:T(8,128)(2,1)S(1)}, bf16[256,1024]{1,0:T(8,128)(2,1)S(1)}, u32[]{:S(2)}, u32[]{:S(2)}) %collective-permute-start.33) | collective-permute-done | bytes 524320 | tf_op jit(solution)/shard_map/ppermute | solution.py:76
  394.1 3.9 collective-permute-done.27.refs_6_
  398.0 1.5 collective-permute-start.29
  401.6 7.0 %collective-permute-done.35.refs_6_ = bf16[256,1024]{1,0:T(8,128)(2,1)S(1)} collective-permute-done((bf16[256,1024]{1,0:T(8,128)(2,1)S(1)}, bf16[256,1024]{1,0:T(8,128)(2,1)S(1)}, u32[]{:S(2)}, u32[]{:S(2)}) %collective-permute-start.35) | collective-permute-done | bytes 524320 | tf_op jit(solution)/shard_map/ppermute | solution.py:76
  412.1 2.8 lay_out.1
  421.7 4.4 %lay_out_wide.1 = (f32[1024,1024]{1,0:T(8,128)}, f32[256,4096]{1,0:T(8,128)}) custom-call(s32[8]{0:T(128)S(1)} %copy-done.17, bf16[256,1024]{1,0:T(8,128)(2,1)S(1)} %pad_maximum_fusion.7.refs_0_, bf16[256,1024]{1,0:T(8,128)(2,1)S(1)} %collective-permute-done.30.refs_1_, bf16[256,1024]{1,0:T(8,128)(2,1)S(1)} %collective-permute-done.31.refs_2_, ...), custom_call_target="tpu_custom_call" | custom-call | bytes 12582912 | tf_op jit(solution)/shard_map/lay_out_wide/pallas_call | solution.py:531
  (259 shorter events, 63.6 us)
Async XLA Ops:
  0.6 5.2 %copy-start.34 = (s32[1,256]{1,0:T(1,128)S(1)}, s32[1,256]{1,0:T(1,128)}, u32[]{:S(2)}) copy-start(s32[1,256]{1,0:T(1,128)} %param.22) | copy-start | bytes 3076
  2.8 26.2 %collective-permute-start.2 = (bf16[2,256,1024]{2,1,0:T(8,128)(2,1)S(1)}, bf16[2,256,1024]{2,1,0:T(8,128)(2,1)S(1)}, u32[]{:S(2)}, u32[]{:S(2)}) collective-permute-start(bf16[2,256,1024]{2,1,0:T(8,128)(2,1)S(1)} %constant_dynamic-update-slice_fusion), channel_id=1, source_target_pairs={{0,2},{1,3},{2,0},{3,1},{4,6},{5,7},{6,4},{7,5},{8,10},{9,11},{10,... | collective-permute-start | bytes 3145736 | tf_op jit(solution)/shard_map/ppermute | solution.py:93
  31.2 10.7 %collective-permute-start.3 = (bf16[2,2,256,1024]{3,2,1,0:T(8,128)(2,1)}, bf16[2,2,256,1024]{3,2,1,0:T(8,128)(2,1)}, u32[]{:S(2)}, u32[]{:S(2)}) collective-permute-start(bf16[2,2,256,1024]{3,2,1,0:T(8,128)(2,1)} %pad_maximum_fusion.3), channel_id=1, source_target_pairs={{0,1},{1,0},{2,3},{3,2},{4,5},{5,4},{6,7},{7,6},{8,9},{9,8},{10,11... | collective-permute-start | bytes 6291464 | tf_op jit(solution)/shard_map/ppermute | solution.py:96
  31.5 6.8 %collective-permute-start = (bf16[16,256]{1,0:T(8,128)(2,1)S(1)}, bf16[16,256]{1,0:T(8,128)(2,1)S(1)}, u32[]{:S(2)}, u32[]{:S(2)}) collective-permute-start(bf16[16,256]{1,0:T(8,128)(2,1)S(1)} %pad.25), channel_id=1, source_target_pairs={{0,2},{1,3},{2,0},{3,1},{4,6},{5,7},{6,4},{7,5},{8,10},{9,11},{10,... | collective-permute-start | bytes 24584 | tf_op jit(solution)/shard_map/ppermute | solution.py:93
  34.5 4.3 %copy-start.37 = (bf16[768]{0:T(1024)(128)(2,1)S(1)}, bf16[768]{0:T(1024)(128)(2,1)}, u32[]{:S(2)}) copy-start(bf16[768]{0:T(1024)(128)(2,1)} %param.25) | copy-start | bytes 4612
  34.5 23.7 %all-to-all-start = ((bf16[4,256,768]{2,1,0:T(8,128)(2,1)}), bf16[4,256,768]{2,1,0:T(8,128)(2,1)S(1)}, u32[]{:S(2)}, u32[]{:S(2)}) async-start(bf16[4,256,768]{2,1,0:T(8,128)(2,1)} %bitcast.226), calls=%async_computation | async-start | bytes 3145728 | tf_op jit(solution)/shard_map/all_to_all | solution.py:586
  38.3 1.6 collective-permute-start.1
  44.8 13.5 %copy-start.8 = (bf16[256,1024]{1,0:T(8,128)(2,1)S(1)}, bf16[256,1024]{1,0:T(8,128)(2,1)}, u32[]{:S(2)}) copy-start(bf16[256,1024]{1,0:T(8,128)(2,1)} %dense_ref.1) | copy-start | bytes 1572868
  58.3 10.7 %copy-start.6 = (bf16[4,256,768]{2,1,0:T(8,128)(2,1)}, bf16[4,256,768]{2,1,0:T(8,128)(2,1)S(1)}, u32[]{:S(2)}) copy-start(bf16[4,256,768]{2,1,0:T(8,128)(2,1)S(1)} %all-to-all-done) | copy-start | bytes 4718596
  74.4 53.9 %all-to-all-start.1 = ((bf16[8,1,256,512]{3,2,1,0:T(8,128)(2,1)}), bf16[8,1,256,512]{3,2,1,0:T(8,128)(2,1)S(1)}, u32[]{:S(2)}, u32[]{:S(2)}) async-start(bf16[8,1,256,512]{3,2,1,0:T(8,128)(2,1)} %bitcast.204), calls=%async_computation.1 | async-start | bytes 4194304 | tf_op jit(solution)/shard_map/all_to_all | solution.py:548
  133.3 35.5 %collective-permute-start.4 = (bf16[256,2048]{1,0:T(8,128)(2,1)}, bf16[256,2048]{1,0:T(8,128)(2,1)}, u32[]{:S(2)}, u32[]{:S(2)}) collective-permute-start(bf16[256,2048]{1,0:T(8,128)(2,1)} %constant_dynamic-slice_fusion.2), channel_id=1, source_target_pairs={{0,2},{1,3},{2,0},{3,1},{4,6},{5,7},{6,4},{7,5},{8,10},{9,11},{10,... | collective-permute-start | bytes 3145736 | tf_op jit(solution)/shard_map/ppermute | solution.py:113
  164.3 61.3 %all-to-all-start.2 = ((bf16[8,1,256,512]{3,2,1,0:T(8,128)(2,1)}), bf16[8,1,256,512]{3,2,1,0:T(8,128)(2,1)}, u32[]{:S(2)}, u32[]{:S(2)}) async-start(bf16[8,1,256,512]{3,2,1,0:T(8,128)(2,1)} %bitcast.32), calls=%async_computation.2 | async-start | bytes 4194304 | tf_op jit(solution)/shard_map/all_to_all | solution.py:631
  170.9 5.6 %copy-start.36 = (bf16[1024]{0:T(1024)(128)(2,1)S(1)}, bf16[1024]{0:T(1024)(128)(2,1)}, u32[]{:S(2)}) copy-start(bf16[1024]{0:T(1024)(128)(2,1)} %param.29) | copy-start | bytes 6148
  172.6 7.8 %collective-permute-start.5 = (bf16[2,256,1024]{2,1,0:T(8,128)(2,1)}, bf16[2,256,1024]{2,1,0:T(8,128)(2,1)}, u32[]{:S(2)}, u32[]{:S(2)}) collective-permute-start(bf16[2,256,1024]{2,1,0:T(8,128)(2,1)} %fusion.20), channel_id=1, source_target_pairs={{0,1},{1,0},{2,3},{3,2},{4,5},{5,4},{6,7},{7,6},{8,9},{9,8},{10,11... | collective-permute-start | bytes 3145736 | tf_op jit(solution)/shard_map/ppermute | solution.py:117
  208.3 13.4 %collective-permute-start.18 = (bf16[128,1024]{1,0:T(8,128)(2,1)S(1)}, bf16[128,1024]{1,0:T(8,128)(2,1)S(1)}, u32[]{:S(2)}, u32[]{:S(2)}) collective-permute-start(bf16[128,1024]{1,0:T(8,128)(2,1)S(1)} %get-tuple-element.89), channel_id=1, source_target_pairs={{8,0},{16,8},{24,16},{28,24},{20,28},{12,20},{4,12},{0,4},{9,1},{1... | collective-permute-start | bytes 786440 | tf_op jit(solution)/shard_map/ppermute | solution.py:52
  213.0 9.6 %collective-permute-start.14 = (bf16[128,1024]{1,0:T(8,128)(2,1)S(1)}, bf16[128,1024]{1,0:T(8,128)(2,1)S(1)}, u32[]{:S(2)}, u32[]{:S(2)}) collective-permute-start(bf16[128,1024]{1,0:T(8,128)(2,1)S(1)} %get-tuple-element.88), channel_id=1, source_target_pairs={{0,8},{8,16},{16,24},{24,28},{28,20},{20,12},{12,4},{4,0},{1,9},{9... | collective-permute-start | bytes 786440 | tf_op jit(solution)/shard_map/ppermute | solution.py:51
  222.5 52.5 %collective-permute-start.19 = (bf16[256,1024]{1,0:T(8,128)(2,1)}, bf16[256,1024]{1,0:T(8,128)(2,1)}, u32[]{:S(2)}, u32[]{:S(2)}) collective-permute-start(bf16[256,1024]{1,0:T(8,128)(2,1)} %pad_maximum_fusion.6), channel_id=1, source_target_pairs={{8,0},{16,8},{24,16},{28,24},{20,28},{12,20},{4,12},{0,4},{9,1},{1... | collective-permute-start | bytes 1572872 | tf_op jit(solution)/shard_map/ppermute | solution.py:63
  223.4 51.7 %collective-permute-start.15 = (bf16[256,1024]{1,0:T(8,128)(2,1)}, bf16[256,1024]{1,0:T(8,128)(2,1)}, u32[]{:S(2)}, u32[]{:S(2)}) collective-permute-start(bf16[256,1024]{1,0:T(8,128)(2,1)} %pad_maximum_fusion.5), channel_id=1, source_target_pairs={{0,8},{8,16},{16,24},{24,28},{28,20},{20,12},{12,4},{4,0},{1,9},{9... | collective-permute-start | bytes 1572872 | tf_op jit(solution)/shard_map/ppermute | solution.py:62
  236.8 5.3 %copy-start.2 = (bf16[1024,256]{1,0:T(8,128)(2,1)S(1)}, bf16[1024,256]{1,0:T(8,128)(2,1)}, u32[]{:S(2)}) copy-start(bf16[1024,256]{1,0:T(8,128)(2,1)} %copy-done.1) | copy-start | bytes 1572868
  236.8 5.3 %copy-start.21 = (bf16[4,1,256,1024]{3,2,1,0:T(8,128)(2,1)S(1)}, bf16[4,1,256,1024]{3,2,1,0:T(8,128)(2,1)}, u32[]{:S(2)}) copy-start(bf16[4,1,256,1024]{3,2,1,0:T(8,128)(2,1)} %slice.231) | copy-start | bytes 6291460
  261.5 4.7 %copy-start.9 = (bf16[256,1024]{1,0:T(8,128)(2,1)S(1)}, bf16[256,1024]{1,0:T(8,128)(2,1)}, u32[]{:S(2)}) copy-start(bf16[256,1024]{1,0:T(8,128)(2,1)} %dense_ref.1) | copy-start | bytes 1572868
  261.5 4.7 %copy-start.28 = (f32[1024,1024]{1,0:T(8,128)S(1)}, f32[1024,1024]{1,0:T(8,128)}, u32[]{:S(2)}) copy-start(f32[1024,1024]{1,0:T(8,128)} %get-tuple-element.32) | copy-start | bytes 12582916
  264.1 15.8 %collective-permute-start.6 = (bf16[272,256]{1,0:T(8,128)(2,1)}, bf16[272,256]{1,0:T(8,128)(2,1)}, u32[]{:S(2)}, u32[]{:S(2)}) collective-permute-start(bf16[272,256]{1,0:T(8,128)(2,1)} %get-tuple-element.80), channel_id=1, source_target_pairs={{0,8},{8,16},{16,24},{24,28},{28,20},{20,12},{12,4},{4,0},{1,9},{9... | collective-permute-start | bytes 417800 | tf_op jit(solution)/shard_map/ppermute | solution.py:51
  264.7 15.2 %collective-permute-start.10 = (bf16[272,256]{1,0:T(8,128)(2,1)}, bf16[272,256]{1,0:T(8,128)(2,1)}, u32[]{:S(2)}, u32[]{:S(2)}) collective-permute-start(bf16[272,256]{1,0:T(8,128)(2,1)} %get-tuple-element.82), channel_id=1, source_target_pairs={{8,0},{16,8},{24,16},{28,24},{20,28},{12,20},{4,12},{0,4},{9,1},{1... | collective-permute-start | bytes 417800 | tf_op jit(solution)/shard_map/ppermute | solution.py:52
  270.2 63.9 %all-to-all-start.3 = ((bf16[4,512,1024]{2,1,0:T(8,128)(2,1)}), bf16[4,512,1024]{2,1,0:T(8,128)(2,1)}, u32[]{:S(2)}, u32[]{:S(2)}) async-start(bf16[4,512,1024]{2,1,0:T(8,128)(2,1)} %pad_maximum_fusion.2), calls=%async_computation.3 | async-start | bytes 8388608 | tf_op jit(solution)/shard_map/all_to_all | solution.py:637
  277.9 23.6 %collective-permute-start.16 = (bf16[256,1024]{1,0:T(8,128)(2,1)}, bf16[256,1024]{1,0:T(8,128)(2,1)S(1)}, u32[]{:S(2)}, u32[]{:S(2)}) collective-permute-start(bf16[256,1024]{1,0:T(8,128)(2,1)} %get-tuple-element.65), channel_id=1, source_target_pairs={{0,8},{8,16},{16,24},{24,28},{28,20},{20,12},{12,4},{4,0},{1,9},{9... | collective-permute-start | bytes 1572872 | tf_op jit(solution)/shard_map/ppermute | solution.py:62
  278.5 23.0 %collective-permute-start.20 = (bf16[256,1024]{1,0:T(8,128)(2,1)}, bf16[256,1024]{1,0:T(8,128)(2,1)}, u32[]{:S(2)}, u32[]{:S(2)}) collective-permute-start(bf16[256,1024]{1,0:T(8,128)(2,1)} %get-tuple-element.66), channel_id=1, source_target_pairs={{8,0},{16,8},{24,16},{28,24},{20,28},{12,20},{4,12},{0,4},{9,1},{1... | collective-permute-start | bytes 1572872 | tf_op jit(solution)/shard_map/ppermute | solution.py:63
  281.8 16.6 %collective-permute-start.7 = (bf16[544,256]{1,0:T(8,128)(2,1)}, bf16[544,256]{1,0:T(8,128)(2,1)}, u32[]{:S(2)}, u32[]{:S(2)}) collective-permute-start(bf16[544,256]{1,0:T(8,128)(2,1)} %pad_maximum_fusion.9), channel_id=1, source_target_pairs={{0,8},{8,16},{16,24},{24,28},{28,20},{20,12},{12,4},{4,0},{1,9},{9... | collective-permute-start | bytes 835592 | tf_op jit(solution)/shard_map/ppermute | solution.py:62
  283.8 22.3 %collective-permute-start.11 = (bf16[544,256]{1,0:T(8,128)(2,1)}, bf16[544,256]{1,0:T(8,128)(2,1)S(1)}, u32[]{:S(2)}, u32[]{:S(2)}) collective-permute-start(bf16[544,256]{1,0:T(8,128)(2,1)} %pad_maximum_fusion.10), channel_id=1, source_target_pairs={{8,0},{16,8},{24,16},{28,24},{20,28},{12,20},{4,12},{0,4},{9,1},{1... | collective-permute-start | bytes 835592 | tf_op jit(solution)/shard_map/ppermute | solution.py:63
  300.2 9.9 %collective-permute-start.8 = (bf16[544,256]{1,0:T(8,128)(2,1)}, bf16[544,256]{1,0:T(8,128)(2,1)}, u32[]{:S(2)}, u32[]{:S(2)}) collective-permute-start(bf16[544,256]{1,0:T(8,128)(2,1)} %bitcast_add_fusion.6), channel_id=1, source_target_pairs={{0,8},{8,16},{16,24},{24,28},{28,20},{20,12},{12,4},{4,0},{1,9},{9... | collective-permute-start | bytes 835592 | tf_op jit(solution)/shard_map/ppermute | solution.py:62
  304.1 23.2 %collective-permute-start.17 = (bf16[256,1024]{1,0:T(8,128)(2,1)}, bf16[256,1024]{1,0:T(8,128)(2,1)S(1)}, u32[]{:S(2)}, u32[]{:S(2)}) collective-permute-start(bf16[256,1024]{1,0:T(8,128)(2,1)} %get-tuple-element.63), channel_id=1, source_target_pairs={{0,8},{8,16},{16,24},{24,28},{28,20},{20,12},{12,4},{4,0},{1,9},{9... | collective-permute-start | bytes 1572872 | tf_op jit(solution)/shard_map/ppermute | solution.py:62
  304.6 22.7 %collective-permute-start.21 = (bf16[256,1024]{1,0:T(8,128)(2,1)}, bf16[256,1024]{1,0:T(8,128)(2,1)S(1)}, u32[]{:S(2)}, u32[]{:S(2)}) collective-permute-start(bf16[256,1024]{1,0:T(8,128)(2,1)} %get-tuple-element.64), channel_id=1, source_target_pairs={{8,0},{16,8},{24,16},{28,24},{20,28},{12,20},{4,12},{0,4},{9,1},{1... | collective-permute-start | bytes 1572872 | tf_op jit(solution)/shard_map/ppermute | solution.py:63
  312.1 11.8 %collective-permute-start.12 = (bf16[544,256]{1,0:T(8,128)(2,1)}, bf16[544,256]{1,0:T(8,128)(2,1)}, u32[]{:S(2)}, u32[]{:S(2)}) collective-permute-start(bf16[544,256]{1,0:T(8,128)(2,1)} %get-tuple-element.77), channel_id=1, source_target_pairs={{8,0},{16,8},{24,16},{28,24},{20,28},{12,20},{4,12},{0,4},{9,1},{1... | collective-permute-start | bytes 835592 | tf_op jit(solution)/shard_map/ppermute | solution.py:63
  314.0 14.8 %collective-permute-start.9 = (bf16[544,256]{1,0:T(8,128)(2,1)}, bf16[544,256]{1,0:T(8,128)(2,1)S(1)}, u32[]{:S(2)}, u32[]{:S(2)}) collective-permute-start(bf16[544,256]{1,0:T(8,128)(2,1)} %get-tuple-element.76), channel_id=1, source_target_pairs={{0,8},{8,16},{16,24},{24,28},{28,20},{20,12},{12,4},{4,0},{1,9},{9... | collective-permute-start | bytes 835592 | tf_op jit(solution)/shard_map/ppermute | solution.py:62
  325.6 7.3 %collective-permute-start.13 = (bf16[544,256]{1,0:T(8,128)(2,1)}, bf16[544,256]{1,0:T(8,128)(2,1)}, u32[]{:S(2)}, u32[]{:S(2)}) collective-permute-start(bf16[544,256]{1,0:T(8,128)(2,1)} %bitcast_add_fusion.5), channel_id=1, source_target_pairs={{8,0},{16,8},{24,16},{28,24},{20,28},{12,20},{4,12},{0,4},{9,1},{1... | collective-permute-start | bytes 835592 | tf_op jit(solution)/shard_map/ppermute | solution.py:63
  334.0 9.1 %copy-start.33 = (bf16[544,256]{1,0:T(8,128)(2,1)}, bf16[544,256]{1,0:T(8,128)(2,1)S(1)}, u32[]{:S(2)}) copy-start(bf16[544,256]{1,0:T(8,128)(2,1)S(1)} %fusion.27) | copy-start | bytes 835588
  337.4 5.5 %copy-start.23 = (bf16[1,256,1024]{2,1,0:T(8,128)(2,1)S(1)}, bf16[1,256,1024]{2,1,0:T(8,128)(2,1)}, u32[]{:S(2)}) copy-start(bf16[1,256,1024]{2,1,0:T(8,128)(2,1)} %param.20) | copy-start | bytes 1572868
  339.5 11.9 %all-to-all-start.4 = ((bf16[4,240,256]{2,1,0:T(8,128)(2,1)}), bf16[4,240,256]{2,1,0:T(8,128)(2,1)S(1)}, u32[]{:S(2)}, u32[]{:S(2)}) async-start(bf16[4,240,256]{2,1,0:T(8,128)(2,1)} %fusion.42), calls=%async_computation.4 | async-start | bytes 983040 | tf_op jit(solution)/shard_map/all_to_all | solution.py:695
  343.2 10.7 %slice-start = ((bf16[544,256]{1,0:T(8,128)(2,1)}), bf16[128,256]{1,0:T(8,128)(2,1)S(1)}, s32[]{:S(2)}) async-start(bf16[544,256]{1,0:T(8,128)(2,1)} %copy-done.33), calls=%async_computation.5 | async-start | bytes 131072 | tf_op jit(solution)/shard_map/slice | solution.py:716
  351.7 21.5 %collective-permute-start.31 = (bf16[256,1024]{1,0:T(8,128)(2,1)S(1)}, bf16[256,1024]{1,0:T(8,128)(2,1)S(1)}, u32[]{:S(2)}, u32[]{:S(2)}) collective-permute-start(bf16[256,1024]{1,0:T(8,128)(2,1)S(1)} %pad_maximum_fusion.7.refs_0_), channel_id=1, source_target_pairs={{8,0},{16,8},{24,16},{28,24},{20,28},{12,20},{4,12},{0,4},{9,1},{1... | collective-permute-start | bytes 1572872 | tf_op jit(solution)/shard_map/ppermute | solution.py:76
  353.3 21.5 %collective-permute-start.30 = (bf16[256,1024]{1,0:T(8,128)(2,1)S(1)}, bf16[256,1024]{1,0:T(8,128)(2,1)S(1)}, u32[]{:S(2)}, u32[]{:S(2)}) collective-permute-start(bf16[256,1024]{1,0:T(8,128)(2,1)S(1)} %pad_maximum_fusion.7.refs_0_), channel_id=1, source_target_pairs={{0,8},{8,16},{16,24},{24,28},{28,20},{20,12},{12,4},{4,0},{1,9},{9... | collective-permute-start | bytes 1572872 | tf_op jit(solution)/shard_map/ppermute | solution.py:75
  353.9 17.3 %collective-permute-start.23 = (bf16[544,256]{1,0:T(8,128)(2,1)S(1)}, bf16[544,256]{1,0:T(8,128)(2,1)S(1)}, u32[]{:S(2)}, u32[]{:S(2)}) collective-permute-start(bf16[544,256]{1,0:T(8,128)(2,1)S(1)} %fusion.44.refs_0_), channel_id=1, source_target_pairs={{8,0},{16,8},{24,16},{28,24},{20,28},{12,20},{4,12},{0,4},{9,1},{1... | collective-permute-start | bytes 835592 | tf_op jit(solution)/shard_map/ppermute | solution.py:76
  355.5 17.3 %collective-permute-start.22 = (bf16[544,256]{1,0:T(8,128)(2,1)S(1)}, bf16[544,256]{1,0:T(8,128)(2,1)S(1)}, u32[]{:S(2)}, u32[]{:S(2)}) collective-permute-start(bf16[544,256]{1,0:T(8,128)(2,1)S(1)} %fusion.44.refs_0_), channel_id=1, source_target_pairs={{0,8},{8,16},{16,24},{24,28},{28,20},{20,12},{12,4},{4,0},{1,9},{9... | collective-permute-start | bytes 835592 | tf_op jit(solution)/shard_map/ppermute | solution.py:75
  362.2 20.7 %copy-start.24 = (bf16[1,256,1024]{2,1,0:T(8,128)(2,1)S(1)}, bf16[1,256,1024]{2,1,0:T(8,128)(2,1)}, u32[]{:S(2)}) copy-start(bf16[1,256,1024]{2,1,0:T(8,128)(2,1)} %param.20) | copy-start | bytes 1572868
  371.2 7.7 %copy-start.12 = (bf16[544,256]{1,0:T(8,128)(2,1)}, bf16[544,256]{1,0:T(8,128)(2,1)S(1)}, u32[]{:S(2)}) copy-start(bf16[544,256]{1,0:T(8,128)(2,1)S(1)} %collective-permute-done.23.refs_2_) | copy-start | bytes 835588
  371.2 9.6 %collective-permute-start.25 = (bf16[544,256]{1,0:T(8,128)(2,1)S(1)}, bf16[544,256]{1,0:T(8,128)(2,1)S(1)}, u32[]{:S(2)}, u32[]{:S(2)}) collective-permute-start(bf16[544,256]{1,0:T(8,128)(2,1)S(1)} %collective-permute-done.23.refs_2_), channel_id=1, source_target_pairs={{8,0},{16,8},{24,16},{28,24},{20,28},{12,20},{4,12},{0,4},{9,1},{1... | collective-permute-start | bytes 835592 | tf_op jit(solution)/shard_map/ppermute | solution.py:76
  372.7 6.3 %copy-start.14 = (bf16[544,256]{1,0:T(8,128)(2,1)}, bf16[544,256]{1,0:T(8,128)(2,1)S(1)}, u32[]{:S(2)}) copy-start(bf16[544,256]{1,0:T(8,128)(2,1)S(1)} %collective-permute-done.22.refs_1_) | copy-start | bytes 835588
  372.7 9.6 %collective-permute-start.24 = (bf16[544,256]{1,0:T(8,128)(2,1)S(1)}, bf16[544,256]{1,0:T(8,128)(2,1)S(1)}, u32[]{:S(2)}, u32[]{:S(2)}) collective-permute-start(bf16[544,256]{1,0:T(8,128)(2,1)S(1)} %collective-permute-done.22.refs_1_), channel_id=1, source_target_pairs={{0,8},{8,16},{16,24},{24,28},{28,20},{20,12},{12,4},{4,0},{1,9},{9... | collective-permute-start | bytes 835592 | tf_op jit(solution)/shard_map/ppermute | solution.py:75
  373.3 18.8 %collective-permute-start.33 = (bf16[256,1024]{1,0:T(8,128)(2,1)S(1)}, bf16[256,1024]{1,0:T(8,128)(2,1)S(1)}, u32[]{:S(2)}, u32[]{:S(2)}) collective-permute-start(bf16[256,1024]{1,0:T(8,128)(2,1)S(1)} %collective-permute-done.31.refs_2_), channel_id=1, source_target_pairs={{8,0},{16,8},{24,16},{28,24},{20,28},{12,20},{4,12},{0,4},{9,1},{1... | collective-permute-start | bytes 1572872 | tf_op jit(solution)/shard_map/ppermute | solution.py:76
  374.8 18.8 %collective-permute-start.32 = (bf16[256,1024]{1,0:T(8,128)(2,1)S(1)}, bf16[256,1024]{1,0:T(8,128)(2,1)S(1)}, u32[]{:S(2)}, u32[]{:S(2)}) collective-permute-start(bf16[256,1024]{1,0:T(8,128)(2,1)S(1)} %collective-permute-done.30.refs_1_), channel_id=1, source_target_pairs={{0,8},{8,16},{16,24},{24,28},{28,20},{20,12},{12,4},{4,0},{1,9},{9... | collective-permute-start | bytes 1572872 | tf_op jit(solution)/shard_map/ppermute | solution.py:75
  379.0 21.2 %copy-start.31 = (bf16[1,256,1024]{2,1,0:T(8,128)(2,1)S(1)}, bf16[1,256,1024]{2,1,0:T(8,128)(2,1)}, u32[]{:S(2)}) copy-start(bf16[1,256,1024]{2,1,0:T(8,128)(2,1)} %param.21) | copy-start | bytes 1572868
  380.8 17.2 %collective-permute-start.27 = (bf16[544,256]{1,0:T(8,128)(2,1)S(1)}, bf16[544,256]{1,0:T(8,128)(2,1)S(1)}, u32[]{:S(2)}, u32[]{:S(2)}) collective-permute-start(bf16[544,256]{1,0:T(8,128)(2,1)S(1)} %collective-permute-done.25.refs_4_), channel_id=1, source_target_pairs={{8,0},{16,8},{24,16},{28,24},{20,28},{12,20},{4,12},{0,4},{9,1},{1... | collective-permute-start | bytes 835592 | tf_op jit(solution)/shard_map/ppermute | solution.py:76
  382.3 17.3 %collective-permute-start.26 = (bf16[544,256]{1,0:T(8,128)(2,1)S(1)}, bf16[544,256]{1,0:T(8,128)(2,1)S(1)}, u32[]{:S(2)}, u32[]{:S(2)}) collective-permute-start(bf16[544,256]{1,0:T(8,128)(2,1)S(1)} %collective-permute-done.24.refs_3_), channel_id=1, source_target_pairs={{0,8},{8,16},{16,24},{24,28},{28,20},{20,12},{12,4},{4,0},{1,9},{9... | collective-permute-start | bytes 835592 | tf_op jit(solution)/shard_map/ppermute | solution.py:75
  392.1 16.5 %collective-permute-start.35 = (bf16[256,1024]{1,0:T(8,128)(2,1)S(1)}, bf16[256,1024]{1,0:T(8,128)(2,1)S(1)}, u32[]{:S(2)}, u32[]{:S(2)}) collective-permute-start(bf16[256,1024]{1,0:T(8,128)(2,1)S(1)} %collective-permute-done.33.refs_4_), channel_id=1, source_target_pairs={{8,0},{16,8},{24,16},{28,24},{20,28},{12,20},{4,12},{0,4},{9,1},{1... | collective-permute-start | bytes 1572872 | tf_op jit(solution)/shard_map/ppermute | solution.py:76
  393.6 8.0 %copy-start.10 = (bf16[256,1024]{1,0:T(8,128)(2,1)}, bf16[256,1024]{1,0:T(8,128)(2,1)S(1)}, u32[]{:S(2)}) copy-start(bf16[256,1024]{1,0:T(8,128)(2,1)S(1)} %collective-permute-done.32.refs_3_) | copy-start | bytes 1572868
  393.6 17.2 %collective-permute-start.34 = (bf16[256,1024]{1,0:T(8,128)(2,1)S(1)}, bf16[256,1024]{1,0:T(8,128)(2,1)S(1)}, u32[]{:S(2)}, u32[]{:S(2)}) collective-permute-start(bf16[256,1024]{1,0:T(8,128)(2,1)S(1)} %collective-permute-done.32.refs_3_), channel_id=1, source_target_pairs={{0,8},{8,16},{16,24},{24,28},{28,20},{20,12},{12,4},{4,0},{1,9},{9... | collective-permute-start | bytes 1572872 | tf_op jit(solution)/shard_map/ppermute | solution.py:75
  398.0 14.0 %collective-permute-start.29 = (bf16[272,256]{1,0:T(8,128)(2,1)S(1)}, bf16[272,256]{1,0:T(8,128)(2,1)S(1)}, u32[]{:S(2)}, u32[]{:S(2)}) collective-permute-start(bf16[272,256]{1,0:T(8,128)(2,1)S(1)} %dynamic_slice.149), channel_id=1, source_target_pairs={{8,0},{16,8},{24,16},{28,24},{20,28},{12,20},{4,12},{0,4},{9,1},{1... | collective-permute-start | bytes 417800 | tf_op jit(solution)/shard_map/ppermute | solution.py:80
  399.6 12.4 %collective-permute-start.28 = (bf16[272,256]{1,0:T(8,128)(2,1)S(1)}, bf16[272,256]{1,0:T(8,128)(2,1)S(1)}, u32[]{:S(2)}, u32[]{:S(2)}) collective-permute-start(bf16[272,256]{1,0:T(8,128)(2,1)S(1)} %dynamic_slice.148), channel_id=1, source_target_pairs={{0,8},{8,16},{16,24},{24,28},{28,20},{20,12},{12,4},{4,0},{1,9},{9... | collective-permute-start | bytes 417800 | tf_op jit(solution)/shard_map/ppermute | solution.py:79
  400.2 11.9 %copy-start.13 = (bf16[544,256]{1,0:T(8,128)(2,1)S(1)}, bf16[544,256]{1,0:T(8,128)(2,1)}, u32[]{:S(2)}) copy-start(bf16[544,256]{1,0:T(8,128)(2,1)} %copy-done.12) | copy-start | bytes 835588
  400.2 11.9 %copy-start.15 = (bf16[544,256]{1,0:T(8,128)(2,1)S(1)}, bf16[544,256]{1,0:T(8,128)(2,1)}, u32[]{:S(2)}) copy-start(bf16[544,256]{1,0:T(8,128)(2,1)} %copy-done.14) | copy-start | bytes 835588
  400.2 11.9 %copy-start.16 = (s32[8]{0:T(128)S(1)}, s32[8]{0:T(128)}, u32[]{:S(2)}) copy-start(s32[8]{0:T(128)} %stack.176.numbers_ref) | copy-start | bytes 100
  409.3 9.8 %collective-permute-start.37 = (bf16[128,1024]{1,0:T(8,128)(2,1)}, bf16[128,1024]{1,0:T(8,128)(2,1)}, u32[]{:S(2)}, u32[]{:S(2)}) collective-permute-start(bf16[128,1024]{1,0:T(8,128)(2,1)} %dynamic_slice.151), channel_id=1, source_target_pairs={{8,0},{16,8},{24,16},{28,24},{20,28},{12,20},{4,12},{0,4},{9,1},{1... | collective-permute-start | bytes 786440 | tf_op jit(solution)/shard_map/ppermute | solution.py:80
  411.5 7.5 %collective-permute-start.36 = (bf16[128,1024]{1,0:T(8,128)(2,1)}, bf16[128,1024]{1,0:T(8,128)(2,1)}, u32[]{:S(2)}, u32[]{:S(2)}) collective-permute-start(bf16[128,1024]{1,0:T(8,128)(2,1)} %dynamic_slice.150), channel_id=1, source_target_pairs={{0,8},{8,16},{16,24},{24,28},{28,20},{20,12},{12,4},{4,0},{1,9},{9... | collective-permute-start | bytes 786440 | tf_op jit(solution)/shard_map/ppermute | solution.py:79
  417.1 9.1 %copy-start.35 = (f32[256]{0:T(256)}, f32[256]{0:T(256)S(1)}, u32[]{:S(2)}) copy-start(f32[256]{0:T(256)S(1)} %reshape_squeeze.31) | copy-start | bytes 3076
  (26 other events, 49.5 us)

commit v2 on v1

--- a/solution.py
+++ b/solution.py
@@ -680,7 +680,7 @@
     dense_rows = dense_blocks * per
     ahead = joint_rows + dense_rows
     gain_rows = jnp.pad(own[ahead : ahead + fsdp][:, None], ((0, 0), (0, 15), (0, 0)))
-    joint_part = lax.dynamic_slice_in_dim(own, nothing(parts), joint_rows, 0)
+    joint_part = own[:joint_rows]
     late_rows = joint_blocks * per + 16
     exchanged = jnp.concatenate(
         [
@@ -745,6 +745,7 @@
             own, "ctx", ctx,
             lambda state, chunk, number, part: (state[0] + [chunk], state[1] + [number]),
             ([], []),
+            nothing(parts),
         )
         joint_total, dense_total, vectors = lay_out(
             jnp.stack(numbers).astype(jnp.int32), chunks, fsdp, joint_blocks, per,

time: 434 us -> 429 us (0.988)
  waiting for transfers between devices: 159 us -> 150 us
    ppermute x6, waiting for transfers between devices: 30.7 us -> 21.1 us  [ring_gather(): down = lax.ppermute(down, axis, back)]
    ppermute x6, waiting for transfers between devices: 0.02 us -> 5.75 us  [ring_gather(): up = lax.ppermute(up, axis, onward)]
    all_to_all x1, waiting for transfers between devices: 8.26 us -> 2.92 us  [per_device(): exchanged = lax.all_to_all(exchanged, 'fsdp', 0, 0)]
    unnamed x99 -> x93, local copies, waits for them, and re-layouts: 22.7 us -> 19.6 us
  transfers between devices with their start and end apart: 43 -> 43, of which waited for: 15 -> 14; matrix products, arithmetic and copies ran while one was open for 21% -> 23% of each run, Pallas kernels for 14% -> 14%
where the time goes in v2:
time: 429 us; the launch traced here: 421 us
  waiting for transfers between devices  150 us (35%)
  Pallas kernels  75 us (17%)
  starting transfers between devices  61.8 us (14%)
  local copies, waits for them, and re-layouts  53.1 us (12%)
  other arithmetic  49.7 us (12%)
  matrix products  16.6 us (4%)
  between operations  15.4 us (4%)
    all_to_all x1, waiting for transfers between devices, spread_out(): lax.all_to_all(part.reshape((ctx, each) + part.shape[1:]), 'ctx', 0, 0)  48 us
    pallas_call x1, Pallas kernels, attend(): pl.pallas_call(functools.partial(attend_kernel, tile, block, unrolled), g...  26.5 us
    pallas_call x1, Pallas kernels, feed(): pl.pallas_call(feed_kernel, grid=(columns // tile,), in_specs=[whole, pl....  24 us
    ppermute x2, waiting for transfers between devices, gather_pairs(): across = lax.ppermute(own, 'fsdp', [(k, k ^ 2) for k in range(4)])  23.1 us
    ppermute x6, waiting for transfers between devices, ring_gather(): down = lax.ppermute(down, axis, back)  21.1 us
    unnamed x93, local copies, waits for them, and re-layouts  19.6 us
    dot_general x4, matrix products, dot(): lax.dot_general(left, right, (((left_dim,), (right_dim,)), ((), ())), pre...  16.6 us
    ppermute x6, waiting for transfers between devices, ring_reduce(): up = lax.ppermute(mine_up, axis, onward)  16.5 us
  transfers between devices with their start and end apart: 43, of which 14 were waited for; matrix products, arithmetic and copies ran while one was open for 23% of the time, Pallas kernels for 14%

profile of v2, /device:TPU:0, one launch (start us, length us, event | category | flops | bytes accessed | tf_op | source)
XLA Modules:
  0.0 421.2 jit_solution(17955048498737629572)
XLA Ops:
  2.8 3.0 collective-permute-start.2
  5.8 23.1 %collective-permute-done.2 = bf16[2,256,1024]{2,1,0:T(8,128)(2,1)S(1)} collective-permute-done((bf16[2,256,1024]{2,1,0:T(8,128)(2,1)S(1)}, bf16[2,256,1024]{2,1,0:T(8,128)(2,1)S(1)}, u32[]{:S(2)}, u32[]{:S(2)}) %collective-permute-start.2) | collective-permute-done | bytes 1048608 | tf_op jit(solution)/shard_map/ppermute | solution.py:93
  29.2 1.5 pad_maximum_fusion.3
  31.5 1.8 collective-permute-start
  34.5 3.7 all-to-all-start
  40.0 1.9 fusion.40
  42.0 2.4 select_bitcast_fusion.1
  44.8 2.5 copy.55
  47.3 11.0 %all-to-all-done = bf16[4,256,768]{2,1,0:T(8,128)(2,1)S(1)} async-done(((bf16[4,256,768]{2,1,0:T(8,128)(2,1)}), bf16[4,256,768]{2,1,0:T(8,128)(2,1)S(1)}, u32[]{:S(2)}, u32[]{:S(2)}) %all-to-all-start) | async-done | bytes 1572896 | tf_op jit(solution)/shard_map/all_to_all | solution.py:586
  58.3 10.7 %project.1 = (bf16[8,256,512]{2,1,0:T(8,128)(2,1)S(1)}, bf16[1024,1024]{1,0:T(8,128)(2,1)S(1)}, bf16[1024,1024]{1,0:T(8,128)(2,1)S(1)}, bf16[1024,1024]{1,0:T(8,128)(2,1)S(1)}) custom-call(bf16[4,2,256,1024]{3,2,1,0:T(8,128)(2,1)} %bitcast.219, bf16[4,2,256,1024]{3,2,1,0:T(8,128)(2,1)} %bitcast.220, f32[4,1024]{1,0:T(4,128)S(1)} %bitcast.208, ...), custom_call_target="tpu_custom_call" | custom-call | flops 3221225472 | bytes 16777216 | tf_op jit(solution)/shard_map/project/pallas_call | solution.py:166
  74.4 5.8 %all-to-all-start.1 = ((bf16[8,1,256,512]{3,2,1,0:T(8,128)(2,1)}), bf16[8,1,256,512]{3,2,1,0:T(8,128)(2,1)S(1)}, u32[]{:S(2)}, u32[]{:S(2)}) async-start(bf16[8,1,256,512]{3,2,1,0:T(8,128)(2,1)} %bitcast.204), calls=%async_computation.1 | async-start | bytes 4194304 | tf_op jit(solution)/shard_map/all_to_all | solution.py:548
  80.2 48.0 %all-to-all-done.1 = bf16[8,1,256,512]{3,2,1,0:T(8,128)(2,1)S(1)} async-done(((bf16[8,1,256,512]{3,2,1,0:T(8,128)(2,1)}), bf16[8,1,256,512]{3,2,1,0:T(8,128)(2,1)S(1)}, u32[]{:S(2)}, u32[]{:S(2)}) %all-to-all-start.1) | async-done | bytes 2097184 | tf_op jit(solution)/shard_map/all_to_all | solution.py:548
  130.5 2.8 constant_dynamic-slice_fusion.3
  134.0 26.5 %attend.1 = bf16[2048,512]{1,0:T(8,128)(2,1)} custom-call(s32[16]{0:T(128)S(1)} %fusion.63.order_ref, bf16[2048,512]{1,0:T(8,128)(2,1)S(1)} %bitcast.203, bf16[8,256,512]{2,1,0:T(8,128)(2,1)S(1)} %copy-done.4), custom_call_target="tpu_custom_call" | custom-call | flops 30064771072 | bytes 4194304 | tf_op jit(solution)/shard_map/attend/pallas_call | solution.py:347
  160.4 2.7 copy.72
  164.3 4.5 %all-to-all-start.2 = ((bf16[8,1,256,512]{3,2,1,0:T(8,128)(2,1)}), bf16[8,1,256,512]{3,2,1,0:T(8,128)(2,1)}, u32[]{:S(2)}, u32[]{:S(2)}) async-start(bf16[8,1,256,512]{3,2,1,0:T(8,128)(2,1)} %bitcast.32), calls=%async_computation.2 | async-start | bytes 4194304 | tf_op jit(solution)/shard_map/all_to_all | solution.py:631
  168.8 2.0 select_bitcast_fusion.4
  170.9 1.7 fusion.20
  176.6 3.2 slice.235
  180.4 1.8 select_bitcast_fusion.3
  182.3 1.5 copy.58
  183.9 24.0 %feed.1 = (bf16[1024,1024]{1,0:T(8,128)(2,1)S(1)}, bf16[1024,1024]{1,0:T(8,128)(2,1)S(1)}, f32[1,1024]{1,0:T(1,128)S(1)}, f32[1024,1024]{1,0:T(8,128)}, f32[1024,1024]{1,0:T(8,128)}) custom-call(bf16[1024,1024]{1,0:T(8,128)(2,1)} %copy-done.5, bf16[1024,1024]{1,0:T(8,128)(2,1)} %bitcast.225, bf16[1,1024]{1,0:T(2,128)(2,1)S(1)} %broadcast_in_dim.56.bias_ref, ...), custom_call_target="tpu_custom_call" | custom-call | tf_op jit(solution)/shard_map/feed/pallas_call | solution.py:409
  208.3 1.9 collective-permute-start.18
  210.3 2.7 pad_maximum_fusion.first_ref
  214.1 7.6 %collective-permute-done.18 = bf16[128,1024]{1,0:T(8,128)(2,1)S(1)} collective-permute-done((bf16[128,1024]{1,0:T(8,128)(2,1)S(1)}, bf16[128,1024]{1,0:T(8,128)(2,1)S(1)}, u32[]{:S(2)}, u32[]{:S(2)}) %collective-permute-start.18) | collective-permute-done | bytes 262176 | tf_op jit(solution)/shard_map/ppermute | solution.py:52
  223.4 2.2 collective-permute-start.15
  225.6 2.2 copy-done
  227.8 5.3 %unturn.1 = (bf16[1024,768]{1,0:T(8,128)(2,1)S(1)}, bf16[1024,256]{1,0:T(8,128)(2,1)S(1)}) custom-call(bf16[8,256,512]{2,1,0:T(8,128)(2,1)} %bitcast.33.back_ref, f32[1024,128]{1,0:T(8,128)S(1)} %get-tuple-element.103.cos_ref, f32[1024,128]{1,0:T(8,128)S(1)} %get-tuple-element.102.sin_ref, bf16[8,256,1024]{2,1,0:T(8,128)(2,1)S(1)} %copy-done), custom_call_target="tpu_custom_call" | custom-call | flops 8388608 | bytes 5242880 | tf_op jit(solution)/shard_map/unturn/pallas_call | solution.py:212
  235.1 1.7 reduce.5
  236.8 5.2 %convolution_convert_fusion = bf16[1024,768]{1,0:T(8,128)(2,1)} fusion(bf16[1024,1024]{1,0:T(8,128)(2,1)} %copy-done.16, bf16[1024,768]{1,0:T(8,128)(2,1)} %copy-done.7), kind=kOutput, calls=%fused_computation.47 | convolution fusion | flops 1611399168 | bytes 5242880 | tf_op jit(solution)/shard_map/dot_general | solution.py:26
  245.2 7.6 %fusion.2 = (bf16[1024]{0:T(1024)(128)(2,1)S(1)}, bf16[1024]{0:T(1024)(128)(2,1)S(1)}, bf16[1024]{0:T(1024)(128)(2,1)S(1)}, bf16[1024]{0:T(1024)(128)(2,1)S(1)}, bf16[1024,1024]{1,0:T(8,128)(2,1)}) fusion(bf16[1024,1024]{1,0:T(8,128)(2,1)} %copy-done.15, f32[1024,1024]{1,0:T(8,128)} %get-tuple-element.37, f32[1024]{0:T(1024)S(1)} %bitcast.244, ...), kind=kOutput, calls=%fused_computation.25 | convolution fusion | flops 1622142976 | bytes 11550720 | tf_op jit(solution)/shard_map/dot_general | solution.py:26
  253.3 5.3 %reshape.386 = bf16[4,8,32,3,256]{4,3,2,1,0:T(4,128)(2,1)} reshape(bf16[1024,768]{1,0:T(8,128)(2,1)} %convolution_convert_fusion) | data formatting | bytes 3145728 | tf_op jit(solution)/shard_map/reshape | solution.py:669
  258.5 2.0 copy.61
  261.8 1.4 collective-permute-start.10
  263.3 2.6 bitcast_add_fusion.2
  266.5 1.4 collective-permute-start.20
  270.7 1.4 collective-permute-start.11
  272.1 12.8 %collective-permute-done.7 = bf16[544,256]{1,0:T(8,128)(2,1)} collective-permute-done((bf16[544,256]{1,0:T(8,128)(2,1)}, bf16[544,256]{1,0:T(8,128)(2,1)}, u32[]{:S(2)}, u32[]{:S(2)}) %collective-permute-start.7) | collective-permute-done | bytes 278560 | tf_op jit(solution)/shard_map/ppermute | solution.py:62
  285.0 1.8 bitcast_add_fusion.6
  287.8 2.8 bitcast_add_fusion.3
  292.6 3.7 collective-permute-done.8
  296.3 2.0 bitcast_add_fusion.7
  300.2 2.1 collective-permute-start.9
  302.3 6.5 %collective-permute-done.12 = bf16[544,256]{1,0:T(8,128)(2,1)} collective-permute-done((bf16[544,256]{1,0:T(8,128)(2,1)}, bf16[544,256]{1,0:T(8,128)(2,1)}, u32[]{:S(2)}, u32[]{:S(2)}) %collective-permute-start.12) | collective-permute-done | bytes 278560 | tf_op jit(solution)/shard_map/ppermute | solution.py:63
  308.8 1.8 bitcast_add_fusion.5
  312.7 1.5 fusion.23
  314.5 2.9 collective-permute-done.13
  319.5 3.5 all-to-all-start.4
  323.0 3.0 add_convert_fusion.1
  326.0 2.5 pad_maximum_fusion.2
  328.5 2.9 all-to-all-done.4
  331.4 4.9 %all-to-all-start.3 = ((bf16[4,512,1024]{2,1,0:T(8,128)(2,1)}), bf16[4,512,1024]{2,1,0:T(8,128)(2,1)}, u32[]{:S(2)}, u32[]{:S(2)}) async-start(bf16[4,512,1024]{2,1,0:T(8,128)(2,1)} %pad_maximum_fusion.2), calls=%async_computation.3 | async-start | bytes 8388608 | tf_op jit(solution)/shard_map/all_to_all | solution.py:637
  341.2 15.8 %collective-permute-done.23.refs_2_ = bf16[544,256]{1,0:T(8,128)(2,1)S(1)} collective-permute-done((bf16[544,256]{1,0:T(8,128)(2,1)S(1)}, bf16[544,256]{1,0:T(8,128)(2,1)S(1)}, u32[]{:S(2)}, u32[]{:S(2)}) %collective-permute-start.23) | collective-permute-done | bytes 278560 | tf_op jit(solution)/shard_map/ppermute | solution.py:76
  358.4 1.8 collective-permute-start.33
  361.3 5.3 %collective-permute-done.25.refs_4_ = bf16[544,256]{1,0:T(8,128)(2,1)} collective-permute-done((bf16[544,256]{1,0:T(8,128)(2,1)S(1)}, bf16[544,256]{1,0:T(8,128)(2,1)}, u32[]{:S(2)}, u32[]{:S(2)}) %collective-permute-start.25) | collective-permute-done | bytes 278560 | tf_op jit(solution)/shard_map/ppermute | solution.py:76
  373.6 5.7 %collective-permute-done.24.refs_3_ = bf16[544,256]{1,0:T(8,128)(2,1)} collective-permute-done((bf16[544,256]{1,0:T(8,128)(2,1)S(1)}, bf16[544,256]{1,0:T(8,128)(2,1)}, u32[]{:S(2)}, u32[]{:S(2)}) %collective-permute-start.24) | collective-permute-done | bytes 278560 | tf_op jit(solution)/shard_map/ppermute | solution.py:75
  379.6 1.7 collective-permute-start.35
  381.7 2.9 all-to-all-done.3
  384.5 3.3 copy.73
  391.0 5.0 %convert_reduce_fusion = (f32[256]{0:T(256)S(1)}, f32[256,1024]{1,0:T(8,128)}, f32[256,1024]{1,0:T(8,128)}) fusion(bf16[4,512,1024]{2,1,0:T(8,128)(2,1)} %all-to-all-done.3), kind=kLoop, calls=%fused_computation.21 | loop fusion | flops 4718336 | bytes 6292480 | tf_op jit(solution)/shard_map/reduce_sum | solution.py:771
  396.8 1.7 fusion.19
  398.6 2.8 fusion.13
  405.8 3.3 lay_out.1
  415.1 5.1 %lay_out_wide.1 = (f32[1024,1024]{1,0:T(8,128)}, f32[256,4096]{1,0:T(8,128)}) custom-call(s32[8]{0:T(128)S(1)} %stack.176.numbers_ref, bf16[256,1024]{1,0:T(8,128)(2,1)S(1)} %pad_maximum_fusion.7.refs_0_, bf16[256,1024]{1,0:T(8,128)(2,1)S(1)} %collective-permute-done.30.refs_1_, bf16[256,1024]{1,0:T(8,128)(2,1)S(1)} %collective-permute-done.31.refs_2_, ...), custom_call_target="tpu_custom_call" | custom-call | bytes 12582912 | tf_op jit(solution)/shard_map/lay_out_wide/pallas_call | solution.py:531
  (253 shorter events, 60.0 us)
Async XLA Ops:
  0.6 5.2 %copy-start.31 = (s32[1,256]{1,0:T(1,128)S(1)}, s32[1,256]{1,0:T(1,128)}, u32[]{:S(2)}) copy-start(s32[1,256]{1,0:T(1,128)} %param.22) | copy-start | bytes 3076
  2.8 26.2 %collective-permute-start.2 = (bf16[2,256,1024]{2,1,0:T(8,128)(2,1)S(1)}, bf16[2,256,1024]{2,1,0:T(8,128)(2,1)S(1)}, u32[]{:S(2)}, u32[]{:S(2)}) collective-permute-start(bf16[2,256,1024]{2,1,0:T(8,128)(2,1)S(1)} %constant_dynamic-update-slice_fusion), channel_id=1, source_target_pairs={{0,2},{1,3},{2,0},{3,1},{4,6},{5,7},{6,4},{7,5},{8,10},{9,11},{10,... | collective-permute-start | bytes 3145736 | tf_op jit(solution)/shard_map/ppermute | solution.py:93
  29.2 4.1 copy-start.28
  31.2 10.7 %collective-permute-start.3 = (bf16[2,2,256,1024]{3,2,1,0:T(8,128)(2,1)}, bf16[2,2,256,1024]{3,2,1,0:T(8,128)(2,1)}, u32[]{:S(2)}, u32[]{:S(2)}) collective-permute-start(bf16[2,2,256,1024]{3,2,1,0:T(8,128)(2,1)} %pad_maximum_fusion.3), channel_id=1, source_target_pairs={{0,1},{1,0},{2,3},{3,2},{4,5},{5,4},{6,7},{7,6},{8,9},{9,8},{10,11... | collective-permute-start | bytes 6291464 | tf_op jit(solution)/shard_map/ppermute | solution.py:96
  31.5 6.8 %collective-permute-start = (bf16[16,256]{1,0:T(8,128)(2,1)S(1)}, bf16[16,256]{1,0:T(8,128)(2,1)S(1)}, u32[]{:S(2)}, u32[]{:S(2)}) collective-permute-start(bf16[16,256]{1,0:T(8,128)(2,1)S(1)} %pad.25), channel_id=1, source_target_pairs={{0,2},{1,3},{2,0},{3,1},{4,6},{5,7},{6,4},{7,5},{8,10},{9,11},{10,... | collective-permute-start | bytes 24584 | tf_op jit(solution)/shard_map/ppermute | solution.py:93
  34.5 4.3 %copy-start.34 = (bf16[768]{0:T(1024)(128)(2,1)S(1)}, bf16[768]{0:T(1024)(128)(2,1)}, u32[]{:S(2)}) copy-start(bf16[768]{0:T(1024)(128)(2,1)} %param.25) | copy-start | bytes 4612
  34.5 23.7 %all-to-all-start = ((bf16[4,256,768]{2,1,0:T(8,128)(2,1)}), bf16[4,256,768]{2,1,0:T(8,128)(2,1)S(1)}, u32[]{:S(2)}, u32[]{:S(2)}) async-start(bf16[4,256,768]{2,1,0:T(8,128)(2,1)} %bitcast.226), calls=%async_computation | async-start | bytes 3145728 | tf_op jit(solution)/shard_map/all_to_all | solution.py:586
  38.3 1.6 collective-permute-start.1
  44.8 13.5 %copy-start.8 = (bf16[256,1024]{1,0:T(8,128)(2,1)S(1)}, bf16[256,1024]{1,0:T(8,128)(2,1)}, u32[]{:S(2)}) copy-start(bf16[256,1024]{1,0:T(8,128)(2,1)} %dense_ref.1) | copy-start | bytes 1572868
  58.3 10.7 %copy-start.6 = (bf16[4,256,768]{2,1,0:T(8,128)(2,1)}, bf16[4,256,768]{2,1,0:T(8,128)(2,1)S(1)}, u32[]{:S(2)}) copy-start(bf16[4,256,768]{2,1,0:T(8,128)(2,1)S(1)} %all-to-all-done) | copy-start | bytes 4718596
  74.4 53.9 %all-to-all-start.1 = ((bf16[8,1,256,512]{3,2,1,0:T(8,128)(2,1)}), bf16[8,1,256,512]{3,2,1,0:T(8,128)(2,1)S(1)}, u32[]{:S(2)}, u32[]{:S(2)}) async-start(bf16[8,1,256,512]{3,2,1,0:T(8,128)(2,1)} %bitcast.204), calls=%async_computation.1 | async-start | bytes 4194304 | tf_op jit(solution)/shard_map/all_to_all | solution.py:548
  130.5 3.4 copy-start.4
  133.3 35.5 %collective-permute-start.4 = (bf16[256,2048]{1,0:T(8,128)(2,1)}, bf16[256,2048]{1,0:T(8,128)(2,1)}, u32[]{:S(2)}, u32[]{:S(2)}) collective-permute-start(bf16[256,2048]{1,0:T(8,128)(2,1)} %constant_dynamic-slice_fusion.3), channel_id=1, source_target_pairs={{0,2},{1,3},{2,0},{3,1},{4,6},{5,7},{6,4},{7,5},{8,10},{9,11},{10,... | collective-permute-start | bytes 3145736 | tf_op jit(solution)/shard_map/ppermute | solution.py:113
  164.3 61.4 %all-to-all-start.2 = ((bf16[8,1,256,512]{3,2,1,0:T(8,128)(2,1)}), bf16[8,1,256,512]{3,2,1,0:T(8,128)(2,1)}, u32[]{:S(2)}, u32[]{:S(2)}) async-start(bf16[8,1,256,512]{3,2,1,0:T(8,128)(2,1)} %bitcast.32), calls=%async_computation.2 | async-start | bytes 4194304 | tf_op jit(solution)/shard_map/all_to_all | solution.py:631
  170.9 5.6 %copy-start.33 = (bf16[1024]{0:T(1024)(128)(2,1)S(1)}, bf16[1024]{0:T(1024)(128)(2,1)}, u32[]{:S(2)}) copy-start(bf16[1024]{0:T(1024)(128)(2,1)} %param.29) | copy-start | bytes 6148
  172.6 7.8 %collective-permute-start.5 = (bf16[2,256,1024]{2,1,0:T(8,128)(2,1)}, bf16[2,256,1024]{2,1,0:T(8,128)(2,1)}, u32[]{:S(2)}, u32[]{:S(2)}) collective-permute-start(bf16[2,256,1024]{2,1,0:T(8,128)(2,1)} %fusion.20), channel_id=1, source_target_pairs={{0,1},{1,0},{2,3},{3,2},{4,5},{5,4},{6,7},{7,6},{8,9},{9,8},{10,11... | collective-permute-start | bytes 3145736 | tf_op jit(solution)/shard_map/ppermute | solution.py:117
  176.5 3.3 copy-start.20
  208.3 13.4 %collective-permute-start.18 = (bf16[128,1024]{1,0:T(8,128)(2,1)S(1)}, bf16[128,1024]{1,0:T(8,128)(2,1)S(1)}, u32[]{:S(2)}, u32[]{:S(2)}) collective-permute-start(bf16[128,1024]{1,0:T(8,128)(2,1)S(1)} %get-tuple-element.89), channel_id=1, source_target_pairs={{8,0},{16,8},{24,16},{28,24},{20,28},{12,20},{4,12},{0,4},{9,1},{1... | collective-permute-start | bytes 786440 | tf_op jit(solution)/shard_map/ppermute | solution.py:52
  213.0 9.6 %collective-permute-start.14 = (bf16[128,1024]{1,0:T(8,128)(2,1)S(1)}, bf16[128,1024]{1,0:T(8,128)(2,1)S(1)}, u32[]{:S(2)}, u32[]{:S(2)}) collective-permute-start(bf16[128,1024]{1,0:T(8,128)(2,1)S(1)} %get-tuple-element.88), channel_id=1, source_target_pairs={{0,8},{8,16},{16,24},{24,28},{28,20},{20,12},{12,4},{4,0},{1,9},{9... | collective-permute-start | bytes 786440 | tf_op jit(solution)/shard_map/ppermute | solution.py:51
  222.6 40.7 %collective-permute-start.19 = (bf16[256,1024]{1,0:T(8,128)(2,1)}, bf16[256,1024]{1,0:T(8,128)(2,1)}, u32[]{:S(2)}, u32[]{:S(2)}) collective-permute-start(bf16[256,1024]{1,0:T(8,128)(2,1)} %pad_maximum_fusion.6), channel_id=1, source_target_pairs={{8,0},{16,8},{24,16},{28,24},{20,28},{12,20},{4,12},{0,4},{9,1},{1... | collective-permute-start | bytes 1572872 | tf_op jit(solution)/shard_map/ppermute | solution.py:63
  223.4 39.8 %collective-permute-start.15 = (bf16[256,1024]{1,0:T(8,128)(2,1)}, bf16[256,1024]{1,0:T(8,128)(2,1)}, u32[]{:S(2)}, u32[]{:S(2)}) collective-permute-start(bf16[256,1024]{1,0:T(8,128)(2,1)} %pad_maximum_fusion.5), channel_id=1, source_target_pairs={{0,8},{8,16},{16,24},{24,28},{28,20},{20,12},{12,4},{4,0},{1,9},{9... | collective-permute-start | bytes 1572872 | tf_op jit(solution)/shard_map/ppermute | solution.py:62
  236.8 5.3 %copy-start.2 = (bf16[1024,256]{1,0:T(8,128)(2,1)S(1)}, bf16[1024,256]{1,0:T(8,128)(2,1)}, u32[]{:S(2)}) copy-start(bf16[1024,256]{1,0:T(8,128)(2,1)} %copy-done.1) | copy-start | bytes 1572868
  236.8 5.3 %copy-start.19 = (bf16[4,1,256,1024]{3,2,1,0:T(8,128)(2,1)S(1)}, bf16[4,1,256,1024]{3,2,1,0:T(8,128)(2,1)}, u32[]{:S(2)}) copy-start(bf16[4,1,256,1024]{3,2,1,0:T(8,128)(2,1)} %slice.235) | copy-start | bytes 6291460
  261.1 6.8 %copy-start.26 = (bf16[8,544,256]{2,1,0:T(8,128)(2,1)}, bf16[8,544,256]{2,1,0:T(8,128)(2,1)S(1)}, u32[]{:S(2)}) copy-start(bf16[8,544,256]{2,1,0:T(8,128)(2,1)S(1)} %fusion.5) | copy-start | bytes 6684676
  261.2 6.7 %collective-permute-start.6 = (bf16[272,256]{1,0:T(8,128)(2,1)S(1)}, bf16[272,256]{1,0:T(8,128)(2,1)S(1)}, u32[]{:S(2)}, u32[]{:S(2)}) collective-permute-start(bf16[272,256]{1,0:T(8,128)(2,1)S(1)} %get-tuple-element.80), channel_id=1, source_target_pairs={{0,8},{8,16},{16,24},{24,28},{28,20},{20,12},{12,4},{4,0},{1,9},{9... | collective-permute-start | bytes 417800 | tf_op jit(solution)/shard_map/ppermute | solution.py:51
  261.8 6.1 %collective-permute-start.10 = (bf16[272,256]{1,0:T(8,128)(2,1)S(1)}, bf16[272,256]{1,0:T(8,128)(2,1)S(1)}, u32[]{:S(2)}, u32[]{:S(2)}) collective-permute-start(bf16[272,256]{1,0:T(8,128)(2,1)S(1)} %get-tuple-element.82), channel_id=1, source_target_pairs={{8,0},{16,8},{24,16},{28,24},{20,28},{12,20},{4,12},{0,4},{9,1},{1... | collective-permute-start | bytes 417800 | tf_op jit(solution)/shard_map/ppermute | solution.py:52
  265.9 21.9 %collective-permute-start.16 = (bf16[256,1024]{1,0:T(8,128)(2,1)}, bf16[256,1024]{1,0:T(8,128)(2,1)}, u32[]{:S(2)}, u32[]{:S(2)}) collective-permute-start(bf16[256,1024]{1,0:T(8,128)(2,1)} %get-tuple-element.65), channel_id=1, source_target_pairs={{0,8},{8,16},{16,24},{24,28},{28,20},{20,12},{12,4},{4,0},{1,9},{9... | collective-permute-start | bytes 1572872 | tf_op jit(solution)/shard_map/ppermute | solution.py:62
  266.5 21.3 %collective-permute-start.20 = (bf16[256,1024]{1,0:T(8,128)(2,1)}, bf16[256,1024]{1,0:T(8,128)(2,1)}, u32[]{:S(2)}, u32[]{:S(2)}) collective-permute-start(bf16[256,1024]{1,0:T(8,128)(2,1)} %get-tuple-element.66), channel_id=1, source_target_pairs={{8,0},{16,8},{24,16},{28,24},{20,28},{12,20},{4,12},{0,4},{9,1},{1... | collective-permute-start | bytes 1572872 | tf_op jit(solution)/shard_map/ppermute | solution.py:63
  268.7 16.2 %collective-permute-start.7 = (bf16[544,256]{1,0:T(8,128)(2,1)}, bf16[544,256]{1,0:T(8,128)(2,1)}, u32[]{:S(2)}, u32[]{:S(2)}) collective-permute-start(bf16[544,256]{1,0:T(8,128)(2,1)} %pad_maximum_fusion.9), channel_id=1, source_target_pairs={{0,8},{8,16},{16,24},{24,28},{28,20},{20,12},{12,4},{4,0},{1,9},{9... | collective-permute-start | bytes 835592 | tf_op jit(solution)/shard_map/ppermute | solution.py:62
  270.7 21.8 %collective-permute-start.11 = (bf16[544,256]{1,0:T(8,128)(2,1)}, bf16[544,256]{1,0:T(8,128)(2,1)S(1)}, u32[]{:S(2)}, u32[]{:S(2)}) collective-permute-start(bf16[544,256]{1,0:T(8,128)(2,1)} %pad_maximum_fusion.10), channel_id=1, source_target_pairs={{8,0},{16,8},{24,16},{28,24},{20,28},{12,20},{4,12},{0,4},{9,1},{1... | collective-permute-start | bytes 835592 | tf_op jit(solution)/shard_map/ppermute | solution.py:63
  286.7 9.5 %collective-permute-start.8 = (bf16[544,256]{1,0:T(8,128)(2,1)}, bf16[544,256]{1,0:T(8,128)(2,1)}, u32[]{:S(2)}, u32[]{:S(2)}) collective-permute-start(bf16[544,256]{1,0:T(8,128)(2,1)} %bitcast_add_fusion.6), channel_id=1, source_target_pairs={{0,8},{8,16},{16,24},{24,28},{28,20},{20,12},{12,4},{4,0},{1,9},{9... | collective-permute-start | bytes 835592 | tf_op jit(solution)/shard_map/ppermute | solution.py:62
  290.5 21.4 %collective-permute-start.17 = (bf16[256,1024]{1,0:T(8,128)(2,1)}, bf16[256,1024]{1,0:T(8,128)(2,1)S(1)}, u32[]{:S(2)}, u32[]{:S(2)}) collective-permute-start(bf16[256,1024]{1,0:T(8,128)(2,1)} %get-tuple-element.63), channel_id=1, source_target_pairs={{0,8},{8,16},{16,24},{24,28},{28,20},{20,12},{12,4},{4,0},{1,9},{9... | collective-permute-start | bytes 1572872 | tf_op jit(solution)/shard_map/ppermute | solution.py:62
  291.3 21.4 %collective-permute-start.21 = (bf16[256,1024]{1,0:T(8,128)(2,1)}, bf16[256,1024]{1,0:T(8,128)(2,1)}, u32[]{:S(2)}, u32[]{:S(2)}) collective-permute-start(bf16[256,1024]{1,0:T(8,128)(2,1)} %get-tuple-element.64), channel_id=1, source_target_pairs={{8,0},{16,8},{24,16},{28,24},{20,28},{12,20},{4,12},{0,4},{9,1},{1... | collective-permute-start | bytes 1572872 | tf_op jit(solution)/shard_map/ppermute | solution.py:63
  298.2 10.6 %collective-permute-start.12 = (bf16[544,256]{1,0:T(8,128)(2,1)}, bf16[544,256]{1,0:T(8,128)(2,1)}, u32[]{:S(2)}, u32[]{:S(2)}) collective-permute-start(bf16[544,256]{1,0:T(8,128)(2,1)} %get-tuple-element.77), channel_id=1, source_target_pairs={{8,0},{16,8},{24,16},{28,24},{20,28},{12,20},{4,12},{0,4},{9,1},{1... | collective-permute-start | bytes 835592 | tf_op jit(solution)/shard_map/ppermute | solution.py:63
  300.2 14.3 %collective-permute-start.9 = (bf16[544,256]{1,0:T(8,128)(2,1)}, bf16[544,256]{1,0:T(8,128)(2,1)S(1)}, u32[]{:S(2)}, u32[]{:S(2)}) collective-permute-start(bf16[544,256]{1,0:T(8,128)(2,1)} %get-tuple-element.76), channel_id=1, source_target_pairs={{0,8},{8,16},{16,24},{24,28},{28,20},{20,12},{12,4},{4,0},{1,9},{9... | collective-permute-start | bytes 835592 | tf_op jit(solution)/shard_map/ppermute | solution.py:62
  310.6 6.9 %collective-permute-start.13 = (bf16[544,256]{1,0:T(8,128)(2,1)}, bf16[544,256]{1,0:T(8,128)(2,1)}, u32[]{:S(2)}, u32[]{:S(2)}) collective-permute-start(bf16[544,256]{1,0:T(8,128)(2,1)} %bitcast_add_fusion.5), channel_id=1, source_target_pairs={{8,0},{16,8},{24,16},{28,24},{20,28},{12,20},{4,12},{0,4},{9,1},{1... | collective-permute-start | bytes 835592 | tf_op jit(solution)/shard_map/ppermute | solution.py:63
  314.5 8.5 %copy-start.9 = (bf16[256,1024]{1,0:T(8,128)(2,1)S(1)}, bf16[256,1024]{1,0:T(8,128)(2,1)}, u32[]{:S(2)}) copy-start(bf16[256,1024]{1,0:T(8,128)(2,1)} %dense_ref.1) | copy-start | bytes 1572868
  318.6 17.7 %copy-start.29 = (bf16[544,256]{1,0:T(8,128)(2,1)}, bf16[544,256]{1,0:T(8,128)(2,1)S(1)}, u32[]{:S(2)}) copy-start(bf16[544,256]{1,0:T(8,128)(2,1)S(1)} %fusion.27) | copy-start | bytes 835588
  319.5 11.9 %all-to-all-start.4 = ((bf16[4,240,256]{2,1,0:T(8,128)(2,1)}), bf16[4,240,256]{2,1,0:T(8,128)(2,1)S(1)}, u32[]{:S(2)}, u32[]{:S(2)}) async-start(bf16[4,240,256]{2,1,0:T(8,128)(2,1)} %fusion.42), calls=%async_computation.4 | async-start | bytes 983040 | tf_op jit(solution)/shard_map/all_to_all | solution.py:695
  323.0 3.1 copy-start.27
  331.4 53.1 %all-to-all-start.3 = ((bf16[4,512,1024]{2,1,0:T(8,128)(2,1)}), bf16[4,512,1024]{2,1,0:T(8,128)(2,1)}, u32[]{:S(2)}, u32[]{:S(2)}) async-start(bf16[4,512,1024]{2,1,0:T(8,128)(2,1)} %pad_maximum_fusion.2), calls=%async_computation.3 | async-start | bytes 8388608 | tf_op jit(solution)/shard_map/all_to_all | solution.py:637
  336.3 22.0 %copy-start.21 = (bf16[1,256,1024]{2,1,0:T(8,128)(2,1)S(1)}, bf16[1,256,1024]{2,1,0:T(8,128)(2,1)}, u32[]{:S(2)}) copy-start(bf16[1,256,1024]{2,1,0:T(8,128)(2,1)} %param.20) | copy-start | bytes 1572868
  336.3 2.7 slice-start
  336.7 21.8 %collective-permute-start.31 = (bf16[256,1024]{1,0:T(8,128)(2,1)S(1)}, bf16[256,1024]{1,0:T(8,128)(2,1)S(1)}, u32[]{:S(2)}, u32[]{:S(2)}) collective-permute-start(bf16[256,1024]{1,0:T(8,128)(2,1)S(1)} %pad_maximum_fusion.7.refs_0_), channel_id=1, source_target_pairs={{8,0},{16,8},{24,16},{28,24},{20,28},{12,20},{4,12},{0,4},{9,1},{1... | collective-permute-start | bytes 1572872 | tf_op jit(solution)/shard_map/ppermute | solution.py:76
  338.1 22.2 %collective-permute-start.30 = (bf16[256,1024]{1,0:T(8,128)(2,1)S(1)}, bf16[256,1024]{1,0:T(8,128)(2,1)S(1)}, u32[]{:S(2)}, u32[]{:S(2)}) collective-permute-start(bf16[256,1024]{1,0:T(8,128)(2,1)S(1)} %pad_maximum_fusion.7.refs_0_), channel_id=1, source_target_pairs={{0,8},{8,16},{16,24},{24,28},{28,20},{20,12},{12,4},{4,0},{1,9},{9... | collective-permute-start | bytes 1572872 | tf_op jit(solution)/shard_map/ppermute | solution.py:75
  339.1 17.8 %collective-permute-start.23 = (bf16[544,256]{1,0:T(8,128)(2,1)S(1)}, bf16[544,256]{1,0:T(8,128)(2,1)S(1)}, u32[]{:S(2)}, u32[]{:S(2)}) collective-permute-start(bf16[544,256]{1,0:T(8,128)(2,1)S(1)} %fusion.44.refs_0_), channel_id=1, source_target_pairs={{8,0},{16,8},{24,16},{28,24},{20,28},{12,20},{4,12},{0,4},{9,1},{1... | collective-permute-start | bytes 835592 | tf_op jit(solution)/shard_map/ppermute | solution.py:76
  340.5 20.0 %collective-permute-start.22 = (bf16[544,256]{1,0:T(8,128)(2,1)S(1)}, bf16[544,256]{1,0:T(8,128)(2,1)S(1)}, u32[]{:S(2)}, u32[]{:S(2)}) collective-permute-start(bf16[544,256]{1,0:T(8,128)(2,1)S(1)} %fusion.44.refs_0_), channel_id=1, source_target_pairs={{0,8},{8,16},{16,24},{24,28},{28,20},{20,12},{12,4},{4,0},{1,9},{9... | collective-permute-start | bytes 835592 | tf_op jit(solution)/shard_map/ppermute | solution.py:75
  357.0 4.3 %copy-start.10 = (bf16[544,256]{1,0:T(8,128)(2,1)}, bf16[544,256]{1,0:T(8,128)(2,1)S(1)}, u32[]{:S(2)}) copy-start(bf16[544,256]{1,0:T(8,128)(2,1)S(1)} %collective-permute-done.23.refs_2_) | copy-start | bytes 835588
  357.0 9.7 %collective-permute-start.25 = (bf16[544,256]{1,0:T(8,128)(2,1)S(1)}, bf16[544,256]{1,0:T(8,128)(2,1)}, u32[]{:S(2)}, u32[]{:S(2)}) collective-permute-start(bf16[544,256]{1,0:T(8,128)(2,1)S(1)} %collective-permute-done.23.refs_2_), channel_id=1, source_target_pairs={{8,0},{16,8},{24,16},{28,24},{20,28},{12,20},{4,12},{0,4},{9,1},{1... | collective-permute-start | bytes 835592 | tf_op jit(solution)/shard_map/ppermute | solution.py:76
  358.4 21.2 %collective-permute-start.33 = (bf16[256,1024]{1,0:T(8,128)(2,1)S(1)}, bf16[256,1024]{1,0:T(8,128)(2,1)}, u32[]{:S(2)}, u32[]{:S(2)}) collective-permute-start(bf16[256,1024]{1,0:T(8,128)(2,1)S(1)} %collective-permute-done.31.refs_2_), channel_id=1, source_target_pairs={{8,0},{16,8},{24,16},{28,24},{20,28},{12,20},{4,12},{0,4},{9,1},{1... | collective-permute-start | bytes 1572872 | tf_op jit(solution)/shard_map/ppermute | solution.py:76
  360.2 21.1 %collective-permute-start.32 = (bf16[256,1024]{1,0:T(8,128)(2,1)S(1)}, bf16[256,1024]{1,0:T(8,128)(2,1)}, u32[]{:S(2)}, u32[]{:S(2)}) collective-permute-start(bf16[256,1024]{1,0:T(8,128)(2,1)S(1)} %collective-permute-done.30.refs_1_), channel_id=1, source_target_pairs={{0,8},{8,16},{16,24},{24,28},{28,20},{20,12},{12,4},{4,0},{1,9},{9... | collective-permute-start | bytes 1572872 | tf_op jit(solution)/shard_map/ppermute | solution.py:75
  360.5 13.1 %copy-start.12 = (bf16[544,256]{1,0:T(8,128)(2,1)}, bf16[544,256]{1,0:T(8,128)(2,1)S(1)}, u32[]{:S(2)}) copy-start(bf16[544,256]{1,0:T(8,128)(2,1)S(1)} %collective-permute-done.22.refs_1_) | copy-start | bytes 835588
  360.5 18.8 %collective-permute-start.24 = (bf16[544,256]{1,0:T(8,128)(2,1)S(1)}, bf16[544,256]{1,0:T(8,128)(2,1)}, u32[]{:S(2)}, u32[]{:S(2)}) collective-permute-start(bf16[544,256]{1,0:T(8,128)(2,1)S(1)} %collective-permute-done.22.refs_1_), channel_id=1, source_target_pairs={{0,8},{8,16},{16,24},{24,28},{28,20},{20,12},{12,4},{4,0},{1,9},{9... | collective-permute-start | bytes 835592 | tf_op jit(solution)/shard_map/ppermute | solution.py:75
  366.6 22.4 %collective-permute-start.27 = (bf16[544,256]{1,0:T(8,128)(2,1)}, bf16[544,256]{1,0:T(8,128)(2,1)S(1)}, u32[]{:S(2)}, u32[]{:S(2)}) collective-permute-start(bf16[544,256]{1,0:T(8,128)(2,1)} %collective-permute-done.25.refs_4_), channel_id=1, source_target_pairs={{8,0},{16,8},{24,16},{28,24},{20,28},{12,20},{4,12},{0,4},{9,1},{1... | collective-permute-start | bytes 835592 | tf_op jit(solution)/shard_map/ppermute | solution.py:76
  379.3 16.7 %collective-permute-start.26 = (bf16[544,256]{1,0:T(8,128)(2,1)}, bf16[544,256]{1,0:T(8,128)(2,1)S(1)}, u32[]{:S(2)}, u32[]{:S(2)}) collective-permute-start(bf16[544,256]{1,0:T(8,128)(2,1)} %collective-permute-done.24.refs_3_), channel_id=1, source_target_pairs={{0,8},{8,16},{16,24},{24,28},{28,20},{20,12},{12,4},{4,0},{1,9},{9... | collective-permute-start | bytes 835592 | tf_op jit(solution)/shard_map/ppermute | solution.py:75
  379.6 21.8 %collective-permute-start.35 = (bf16[256,1024]{1,0:T(8,128)(2,1)}, bf16[256,1024]{1,0:T(8,128)(2,1)S(1)}, u32[]{:S(2)}, u32[]{:S(2)}) collective-permute-start(bf16[256,1024]{1,0:T(8,128)(2,1)} %collective-permute-done.33.refs_4_), channel_id=1, source_target_pairs={{8,0},{16,8},{24,16},{28,24},{20,28},{12,20},{4,12},{0,4},{9,1},{1... | collective-permute-start | bytes 1572872 | tf_op jit(solution)/shard_map/ppermute | solution.py:76
  381.4 22.1 %collective-permute-start.34 = (bf16[256,1024]{1,0:T(8,128)(2,1)}, bf16[256,1024]{1,0:T(8,128)(2,1)S(1)}, u32[]{:S(2)}, u32[]{:S(2)}) collective-permute-start(bf16[256,1024]{1,0:T(8,128)(2,1)} %collective-permute-done.32.refs_3_), channel_id=1, source_target_pairs={{0,8},{8,16},{16,24},{24,28},{28,20},{20,12},{12,4},{4,0},{1,9},{9... | collective-permute-start | bytes 1572872 | tf_op jit(solution)/shard_map/ppermute | solution.py:75
  389.7 15.1 %collective-permute-start.29 = (bf16[272,256]{1,0:T(8,128)(2,1)}, bf16[272,256]{1,0:T(8,128)(2,1)}, u32[]{:S(2)}, u32[]{:S(2)}) collective-permute-start(bf16[272,256]{1,0:T(8,128)(2,1)} %constant_dynamic-slice_fusion), channel_id=1, source_target_pairs={{8,0},{16,8},{24,16},{28,24},{20,28},{12,20},{4,12},{0,4},{9,1},{1... | collective-permute-start | bytes 417800 | tf_op jit(solution)/shard_map/ppermute | solution.py:80
  396.1 8.8 %collective-permute-start.28 = (bf16[272,256]{1,0:T(8,128)(2,1)S(1)}, bf16[272,256]{1,0:T(8,128)(2,1)S(1)}, u32[]{:S(2)}, u32[]{:S(2)}) collective-permute-start(bf16[272,256]{1,0:T(8,128)(2,1)S(1)} %constant_dynamic-slice_fusion.1), channel_id=1, source_target_pairs={{0,8},{8,16},{16,24},{24,28},{28,20},{20,12},{12,4},{4,0},{1,9},{9... | collective-permute-start | bytes 417800 | tf_op jit(solution)/shard_map/ppermute | solution.py:79
  398.5 7.3 %copy-start.11 = (bf16[544,256]{1,0:T(8,128)(2,1)S(1)}, bf16[544,256]{1,0:T(8,128)(2,1)}, u32[]{:S(2)}) copy-start(bf16[544,256]{1,0:T(8,128)(2,1)} %copy-done.10) | copy-start | bytes 835588
  398.6 7.3 %copy-start.13 = (bf16[544,256]{1,0:T(8,128)(2,1)S(1)}, bf16[544,256]{1,0:T(8,128)(2,1)}, u32[]{:S(2)}) copy-start(bf16[544,256]{1,0:T(8,128)(2,1)} %copy-done.12) | copy-start | bytes 835588
  402.1 11.9 %collective-permute-start.37 = (bf16[128,1024]{1,0:T(8,128)(2,1)}, bf16[128,1024]{1,0:T(8,128)(2,1)}, u32[]{:S(2)}, u32[]{:S(2)}) collective-permute-start(bf16[128,1024]{1,0:T(8,128)(2,1)} %dynamic_slice.145), channel_id=1, source_target_pairs={{8,0},{16,8},{24,16},{28,24},{20,28},{12,20},{4,12},{0,4},{9,1},{1... | collective-permute-start | bytes 786440 | tf_op jit(solution)/shard_map/ppermute | solution.py:80
  404.2 9.8 %collective-permute-start.36 = (bf16[128,1024]{1,0:T(8,128)(2,1)}, bf16[128,1024]{1,0:T(8,128)(2,1)}, u32[]{:S(2)}, u32[]{:S(2)}) collective-permute-start(bf16[128,1024]{1,0:T(8,128)(2,1)} %dynamic_slice.144), channel_id=1, source_target_pairs={{0,8},{8,16},{16,24},{24,28},{28,20},{20,12},{12,4},{4,0},{1,9},{9... | collective-permute-start | bytes 786440 | tf_op jit(solution)/shard_map/ppermute | solution.py:79
  412.1 8.1 %copy-start.32 = (f32[256]{0:T(256)}, f32[256]{0:T(256)S(1)}, u32[]{:S(2)}) copy-start(f32[256]{0:T(256)S(1)} %reshape_squeeze.31) | copy-start | bytes 3076
  (23 other events, 41.3 us)
